TPU v7x, 512 devices: a whole 4x8x8 slice. The times are simulated.
512 devices in a mesh: mesh: 128 (over y, z, core), sect: 4 (over x).
Axes of the slice: x: 4, y: 8, z: 8, core: 2. Of those that a mesh axis runs over, the one named last changes fastest.
Arguments:
- latent: bfloat16 [65536, 512], P('mesh', 'sect'), may hold values from -6 to 6
- export_rows: int32 [128, 32], P('mesh'), may hold values from 0 to 511, as said below
- halo_slots: int32 [128, 128, 8], P('mesh'), may hold values from 0 to 31
- tile_src: int32 [512, 16], P('mesh'), may hold values from 0 to 11, as said below
- tile_weight: bfloat16 [512, 16, 128, 128], P('mesh'), may hold values from -0.25 to 0.25
- send_w1: bfloat16 [512, 512], replicated, may hold values from -0.25 to 0.25
- send_b1: float32 [512], replicated, may hold values from -3 to 3
- send_w2: bfloat16 [512, 512], P(None, 'sect'), may hold values from -0.25 to 0.25
- send_b2: float32 [512], P('sect'), may hold values from -3 to 3
- node_w1: bfloat16 [1024, 512], replicated, may hold values from -0.1875 to 0.1875
- node_b1: float32 [512], replicated, may hold values from -3 to 3
- node_w2: bfloat16 [512, 512], P(None, 'sect')
- node_b2: bfloat16 [512], P('sect'), may hold values from -3 to 3
- ln_gain: float32 [512], P('sect'), may hold values from 0.5 to 1.5
- ln_bias: float32 [512], P('sect'), may hold values from -3 to 3
Outputs:
- updated: bfloat16 [65536, 512], P('mesh', 'sect')
Inputs may be any that keep to these rules, and one draw needn't show every extreme that they name: `export_rows`: the 32 rows listed for one mesh index are distinct local row numbers of that index. `halo_slots`: each entry names a position in the offered list of mesh index j; repeats may occur. `tile_src`: among the tiles of one mesh index's 4 blocks, every one of the 12 extended blocks is named at least once.
All inputs are finite; a program needn't handle non-finite values.
Results may differ from a plain program's by a relative error of at most 0.008.
Values may be sent and summed in bfloat16 or wider, within the bound.
No kernel may reach another device: no remote copies, remote signals or barrier semaphores. Data moves between devices by JAX's collectives and lax.ppermute only.
A program may use at most 64 MiB of HBM per device.

v0:
```python
import jax
import jax.numpy as jnp
from jax import lax
from jax.sharding import PartitionSpec as P


def local(
    latent,
    export_rows,
    halo_slots,
    tile_src,
    tile_weight,
    send_w1,
    send_b1,
    send_w2,
    send_b2,
    node_w1,
    node_b1,
    node_w2,
    node_b2,
    ln_gain,
    ln_bias,
):
    rows, share = latent.shape
    whole_latent = lax.all_gather(latent, "sect", axis=1, tiled=True)
    width = whole_latent.shape[1]
    send_pre = jnp.dot(whole_latent, send_w1, preferred_element_type=jnp.float32) + send_b1
    hidden_send = jax.nn.silu(send_pre).astype(jnp.bfloat16)
    message = (jnp.dot(hidden_send, send_w2, preferred_element_type=jnp.float32) + send_b2).astype(
        jnp.bfloat16
    )
    offered_rows = export_rows[0]
    slots = halo_slots[0]
    peers = lax.axis_size("mesh")
    offered = message[offered_rows]
    everything = lax.all_gather(offered, "mesh", axis=0, tiled=True)
    flat_index = (
        jnp.arange(peers, dtype=jnp.int32)[:, None] * offered_rows.shape[0] + slots
    ).reshape(-1)
    halo = everything[flat_index]
    tile = tile_weight.shape[-1]
    used = rows + halo.shape[0]
    blocks = (used + tile - 1) // tile
    extended = jnp.concatenate(
        [message, halo, jnp.zeros((blocks * tile - used, share), jnp.bfloat16)], 0
    )
    extended = extended.reshape(blocks, tile, share)
    senders = extended[tile_src]
    summed = jnp.einsum("bkij,bkjc->bic", tile_weight, senders, preferred_element_type=jnp.float32)
    aggregate = summed.reshape(rows, share).astype(jnp.bfloat16)
    whole_aggregate = lax.all_gather(aggregate, "sect", axis=1, tiled=True)
    upper = node_w1[:width]
    lower = node_w1[width:]
    node_pre = jnp.dot(whole_latent, upper, preferred_element_type=jnp.float32)
    node_pre = (
        node_pre + jnp.dot(whole_aggregate, lower, preferred_element_type=jnp.float32) + node_b1
    )
    node_hidden = jax.nn.silu(node_pre).astype(jnp.bfloat16)
    node_out = jnp.dot(node_hidden, node_w2, preferred_element_type=jnp.float32) + node_b2.astype(
        jnp.float32
    )
    total, squares = lax.psum((jnp.sum(node_out, -1), jnp.sum(node_out * node_out, -1)), "sect")
    mean = (total / width)[:, None]
    var = (squares / width)[:, None] - mean * mean
    normed = (node_out - mean) * lax.rsqrt(var + 1e-05)
    return (latent.astype(jnp.float32) + ln_gain * normed + ln_bias).astype(jnp.bfloat16)


def solution(mesh):
    in_specs = (
        P("mesh", "sect"),
        P("mesh", None),
        P("mesh", None, None),
        P("mesh", None),
        P("mesh", None, None, None),
        P(),
        P(),
        P(None, "sect"),
        P("sect"),
        P(),
        P(),
        P(None, "sect"),
        P("sect"),
        P("sect"),
        P("sect"),
    )
    out_specs = P("mesh", "sect")
    return jax.shard_map(local, mesh=mesh, in_specs=in_specs, out_specs=out_specs, check_vma=False)
```

profile of v0, /device:TPU:6, one launch (start us, length us, event | category | flops | bytes accessed | tf_op | source)
XLA Modules:
  0.0 148.7 jit_solution(15313301613453195227)
XLA Ops:
  6.5 16.2 %all_gather.9 = bf16[512,512]{1,0:T(8,128)(2,1)S(1)} all-gather(bf16[512,128]{1,0:T(8,128)(2,1)} %param.15), channel_id=1, replica_groups=mesh['mesh'=128,'sect'=4] {'sect'}, dimensions={1}, use_global_device_ids=true | all-gather | bytes 655360 | tf_op jit(solution)/shard_map/all_gather | solution.py:25
  22.8 0.7 fusion.11
  23.4 0.0 copy-start.4
  23.4 0.0 copy-start.7
  23.5 1.9 %fusion.1 = bf16[512,128]{1,0:T(8,128)(2,1)S(1)} fusion(bf16[512,128]{1,0:T(8,128)(2,1)} %param.22, bf16[512,512]{1,0:T(8,128)(2,1)S(1)} %all_gather.9, bf16[512,512]{1,0:T(8,128)(2,1)} %param.20, f32[512]{0:T(512)} %param.21, f32[128]{0:T(128)} %param.23), kind=kOutput, calls=%fused_computation.9 | convolution fusion | flops 337248256 | bytes 1313280 | tf_op jit(solution)/shard_map/dot_general | solution.py:29
  25.3 1.2 gather_fusion
  26.5 0.0 all-gather.3.cloned.1.call-update
  26.5 0.1 copy.18
  26.7 0.1 add.121
  26.8 0.1 add.122
  26.9 0.1 copy.19
  27.0 0.1 squeeze.7
  27.1 0.1 reshape.98
  27.2 0.6 convert_element_type.34
  27.8 2.5 %fusion.9 = f32[512,512]{1,0:T(8,128)} fusion(bf16[512,512]{1,0:T(8,128)(2,1)S(1)} %all_gather.9, bf16[1024,512]{1,0:T(8,128)(2,1)} %param.24), kind=kOutput, calls=%fused_computation.18 | convolution fusion | flops 268435456 | bytes 2097152 | tf_op jit(solution)/shard_map/dot_general | solution.py:54
  30.3 77.8 %all-gather.3.cloned.1.call-done = bf16[4096,128]{1,0:T(8,128)(2,1)} async-done(((bf16[32,128]{1,0:T(8,128)(2,1)}), bf16[4096,128]{1,0:T(8,128)(2,1)}) %all-gather.3.cloned.1.call-update) | async-done | bytes 1048592 | tf_op jit(solution)/shard_map/all_gather | solution.py:36
  108.0 4.2 %gather_fusion.1 = bf16[1024,128]{1,0:T(8,128)(2,1)S(1)} fusion(bf16[4096,128]{1,0:T(8,128)(2,1)} %all-gather.3.cloned.1.call-done, s32[1024]{0:T(1024)S(1)} %broadcast_clamp_fusion), kind=kCustom, calls=%fused_computation.1 | custom fusion | bytes 528384 | tf_op jit(solution)/shard_map/gather | solution.py:40
  112.3 2.2 %gather_fusion.2 = bf16[64,128,128]{2,1,0:T(8,128)(2,1)} fusion(bf16[12,128,128]{2,1,0:T(8,128)(2,1)S(1)} %bitcast.23, s32[1024]{0:T(1024)S(1)} %pad_clamp_fusion), kind=kCustom, calls=%fused_computation.2 | custom fusion | bytes 4194560 | tf_op jit(solution)/shard_map/gather | solution.py:48
  114.5 2.4 %fusion.2 = bf16[4,128,128]{1,2,0:T(8,128)(2,1)S(1)} fusion(bf16[4,16,128,128]{3,2,1,0:T(8,128)(2,1)S(1)} %copy-done, bf16[4,16,128,128]{3,2,1,0:T(8,128)(2,1)} %bitcast.24), kind=kOutput, calls=%fused_computation.10 | convolution fusion | flops 268500992 | bytes 4325376 | tf_op jit(solution)/shard_map/bkij,bkjc->bic/dot_general | solution.py:49
  116.9 14.4 %all_gather.11 = bf16[512,512]{1,0:T(8,128)(2,1)} all-gather(bf16[512,128]{1,0:T(8,128)(2,1)S(1)} %bitcast.25), channel_id=1, replica_groups=mesh['mesh'=128,'sect'=4] {'sect'}, dimensions={1}, use_global_device_ids=true | all-gather | bytes 655360 | tf_op jit(solution)/shard_map/all_gather | solution.py:51
  131.2 2.1 %fusion.14 = (f32[512]{0:T(512)S(1)}, f32[512]{0:T(512)S(1)}, f32[512,128]{0,1:T(8,128)S(1)}) fusion(f32[128]{0:T(128)} %convert_element_type.34, bf16[512,128]{1,0:T(8,128)(2,1)} %param.26, f32[512,512]{1,0:T(8,128)S(1)} %copy-done.1, bf16[512,512]{1,0:T(8,128)(2,1)} %all_gather.11, f32[512]{0:T(512)} %param.25, bf16[1024,512]{1,0:T(8,128)(2,1)} %param.24), kind=kOutput, calls=%fused_computation.35 | convolution fusion | flops 337640448 | bytes 2497024 | tf_op jit(solution)/shard_map/dot_general | solution.py:59
  133.3 7.6 %all-reduce = (f32[512]{0:T(512)S(1)}, f32[512]{0:T(512)S(1)}) all-reduce(f32[512]{0:T(512)S(1)} %get-tuple-element.6, f32[512]{0:T(512)S(1)} %get-tuple-element.5), channel_id=1, replica_groups=mesh['mesh'=128,'sect'=4] {'sect'}, use_global_device_ids=true, to_apply=%region_3.4 | all-reduce | flops 1024 | bytes 8192 | tf_op jit(solution)/shard_map/psum | solution.py:62
  141.0 0.1 add_convert_fusion
  141.1 0.8 copy.20
  (23 shorter events, 0.1 us)
Async XLA Ops:
  6.5 107.9 %copy-start = (bf16[4,16,128,128]{3,2,1,0:T(8,128)(2,1)S(1)}, bf16[4,16,128,128]{3,2,1,0:T(8,128)(2,1)}, u32[]{:S(2)}) copy-start(bf16[4,16,128,128]{3,2,1,0:T(8,128)(2,1)} %param.19) | copy-start | bytes 6291460
  6.5 101.5 %all-gather.3.cloned.1.call-start = ((), (), s32[]{:S(2)}) async-start(), calls=%async_computation | async-start | bytes 1056768 | tf_op jit(solution)/shard_map/all_gather | solution.py:36
  23.4 3.1 %copy-start.2 = (bf16[512,128]{1,0:T(8,128)(2,1)S(1)}, bf16[512,128]{1,0:T(8,128)(2,1)}, u32[]{:S(2)}) copy-start(bf16[512,128]{1,0:T(8,128)(2,1)} %param.15) | copy-start | bytes 393220
  23.4 3.4 %copy-start.3 = (s32[1,128,8]{1,2,0:T(8,128)S(1)}, s32[1,128,8]{1,2,0:T(8,128)}, u32[]{:S(2)}) copy-start(s32[1,128,8]{1,2,0:T(8,128)} %param.17) | copy-start | bytes 12292
  23.4 3.6 %copy-start.4 = (s32[4,16]{1,0:T(4,128)S(1)}, s32[4,16]{1,0:T(4,128)}, u32[]{:S(2)}) copy-start(s32[4,16]{1,0:T(4,128)} %param.18) | copy-start | bytes 772
  23.4 3.7 %copy-start.7 = (bf16[128]{0:T(256)(128)(2,1)S(1)}, bf16[128]{0:T(256)(128)(2,1)}, u32[]{:S(2)}) copy-start(bf16[128]{0:T(256)(128)(2,1)} %param.27) | copy-start | bytes 772
  114.5 16.7 %copy-start.1 = (f32[512,512]{1,0:T(8,128)S(1)}, f32[512,512]{1,0:T(8,128)}, u32[]{:S(2)}) copy-start(f32[512,512]{1,0:T(8,128)} %fusion.9) | copy-start | bytes 3145732
  131.2 9.8 %copy-start.5 = (f32[128]{0:T(128)S(1)}, f32[128]{0:T(128)}, u32[]{:S(2)}) copy-start(f32[128]{0:T(128)} %param.29) | copy-start | bytes 1540
  131.2 9.8 %copy-start.6 = (f32[128]{0:T(128)S(1)}, f32[128]{0:T(128)}, u32[]{:S(2)}) copy-start(f32[128]{0:T(128)} %param.28) | copy-start | bytes 1540
Sparse Core Ops, SparseCore 0:
  26.7 81.3 all-gather.2
where the time goes:
time: 151 us; the launch traced here: 149 us
  waiting for transfers between devices  77.8 us (52%)
  blocking collectives  38.2 us (25%)
  between operations  13.5 us (9%)
  local copies, waits for them, and re-layouts  8.96 us (6%)
  matrix products  8.81 us (6%)
    all_gather x1, waiting for transfers between devices, local(): everything = lax.all_gather(offered, 'mesh', axis=0, tiled=True)  77.8 us
    all_gather x1, blocking collectives, local(): whole_latent = lax.all_gather(latent, 'sect', axis=1, tiled=True)  16.2 us
    all_gather x1, blocking collectives, local(): whole_aggregate = lax.all_gather(aggregate, 'sect', axis=1, tiled=True)  14.4 us
    psum x1, blocking collectives, local(): lax.psum((jnp.sum(node_out, -1), jnp.sum(node_out * node_out, -1)), 'sect')  7.63 us
    gather x1, local copies, waits for them, and re-layouts, local(): halo = everything[flat_index]  4.24 us
  transfers between devices with their start and end apart: 1, of which 1 were waited for; matrix products, arithmetic and copies ran while one was open for 2% of the time, Pallas kernels for 0%

commit v1 on v0

v1 whole, which is shorter than its diff:
```python
import jax
import jax.numpy as jnp
from jax import lax
from jax.sharding import Mesh
from jax.sharding import PartitionSpec as P

NODE = ("y", "z", "core")
EPS = 1e-05


def send(rows, w1, b1, w2, b2):
    hidden = jnp.dot(rows, w1, preferred_element_type=jnp.float32) + b1
    hidden = jax.nn.silu(hidden).astype(jnp.bfloat16)
    return (jnp.dot(hidden, w2, preferred_element_type=jnp.float32) + b2).astype(jnp.bfloat16)


def pick(index, rows):
    chosen = index[:, None] == jnp.arange(rows.shape[0], dtype=jnp.int32)[None, :]
    chosen = chosen.astype(jnp.bfloat16)
    return jnp.dot(chosen, rows, preferred_element_type=jnp.float32).astype(jnp.bfloat16)


def copies(block, axis):
    peers = lax.axis_size(axis)
    block = jnp.broadcast_to(block[None], (peers,) + block.shape)
    return lax.all_to_all(block, axis, 0, 0)


def local(
    latent,
    export_rows,
    halo_slots,
    tile_src,
    tile_weight,
    send_w1,
    send_b1,
    send_w2,
    send_b2,
    node_w1,
    node_b1,
    node_w2,
    node_b2,
    ln_gain,
    ln_bias,
):
    rows, share = latent.shape
    width = send_w1.shape[0]
    offers = export_rows.shape[1]
    takes = halo_slots.shape[2]
    n_y, n_z, n_core = (lax.axis_size(name) for name in NODE)
    layer = n_z * n_core

    offered_latent = pick(export_rows[0], latent)
    offered_latent = lax.all_gather(offered_latent, "sect", axis=1, tiled=True)
    offered = send(offered_latent, send_w1, send_b1, send_w2, send_b2)
    offered = lax.all_gather(offered, "core", axis=0, tiled=True)
    offered = copies(offered, "z").reshape(layer * offers, share)

    wanted = lax.all_to_all(halo_slots.reshape(n_y, layer * takes), "y", 0, 0, tiled=True)
    wanted = wanted + (jnp.arange(layer * takes, dtype=jnp.int32) // takes * offers)[None, :]
    halo = pick(wanted.reshape(-1), offered)
    halo = lax.all_to_all(halo, "y", 0, 0, tiled=True)

    whole_latent = copies(latent, "sect")
    whole_latent = jnp.concatenate([whole_latent[s] for s in range(width // share)], 1)
    tail = jnp.broadcast_to(node_b2[None], (16, share))
    whole_w2 = copies(jnp.concatenate([node_w2, tail], 0), "sect")
    whole_w2 = jnp.concatenate([whole_w2[s] for s in range(width // share)], 1)
    whole_w2, whole_b2 = whole_w2[:width], whole_w2[width]

    message = send(whole_latent, send_w1, send_b1, send_w2, send_b2)
    tile = tile_weight.shape[-1]
    used = rows + halo.shape[0]
    blocks = (used + tile - 1) // tile
    extended = jnp.concatenate(
        [message, halo, jnp.zeros((blocks * tile - used, share), jnp.bfloat16)], 0
    )
    extended = extended.reshape(blocks, tile, share)
    senders = extended[tile_src]
    summed = jnp.einsum("bkij,bkjc->bic", tile_weight, senders, preferred_element_type=jnp.float32)
    aggregate = summed.reshape(rows, share).astype(jnp.bfloat16)
    whole_aggregate = lax.all_gather(aggregate, "sect", axis=1, tiled=True)

    node_pre = jnp.dot(whole_latent, node_w1[:width], preferred_element_type=jnp.float32)
    node_pre = (
        node_pre
        + jnp.dot(whole_aggregate, node_w1[width:], preferred_element_type=jnp.float32)
        + node_b1
    )
    node_hidden = jax.nn.silu(node_pre).astype(jnp.bfloat16)
    whole_out = jnp.dot(node_hidden, whole_w2, preferred_element_type=jnp.float32)
    whole_out = whole_out + whole_b2.astype(jnp.float32)
    mean = jnp.mean(whole_out, -1, keepdims=True)
    var = jnp.mean(whole_out * whole_out, -1, keepdims=True) - mean * mean
    node_out = jnp.dot(node_hidden, node_w2, preferred_element_type=jnp.float32)
    node_out = node_out + node_b2.astype(jnp.float32)
    normed = (node_out - mean) * lax.rsqrt(var + EPS)
    return (latent.astype(jnp.float32) + ln_gain * normed + ln_bias).astype(jnp.bfloat16)


def solution(mesh):
    n_mesh, n_sect = mesh.devices.shape
    n_y = n_z = int(round((n_mesh // 2) ** 0.5))
    grid = Mesh(mesh.devices.reshape(n_y, n_z, 2, n_sect), NODE + ("sect",))
    in_specs = (
        P(NODE, "sect"),
        P(NODE, None),
        P(NODE, None, None),
        P(NODE, None),
        P(NODE, None, None, None),
        P(),
        P(),
        P(None, "sect"),
        P("sect"),
        P(),
        P(),
        P(None, "sect"),
        P("sect"),
        P("sect"),
        P("sect"),
    )
    out_specs = P(NODE, "sect")
    return jax.shard_map(local, mesh=grid, in_specs=in_specs, out_specs=out_specs, check_vma=False)
```

time: 151 us -> 109 us (0.72)
  waiting for transfers between devices: 77.8 us -> 22.6 us
  starting transfers between devices: 0.01 us -> 35 us
  blocking collectives: 38.2 us -> 23.9 us
  between operations: 13.5 us -> 0.18 us
  matrix products: 8.81 us -> 12.4 us
  other arithmetic: 1.44 us -> 3.55 us
    all_gather x1 -> x0, waiting for transfers between devices: 77.8 us -> none  [local(): everything = lax.all_gather(offered, 'mesh', axis=0, tiled=True)]
    all_to_all x0 -> x5, starting transfers between devices: none -> 35 us  [the longest x3 20.7 us: copies(): return lax.all_to_all(block, axis, 0, 0)]
    all_to_all x0 -> x5, waiting for transfers between devices: none -> 22.6 us  [the longest x3 12.2 us: copies(): return lax.all_to_all(block, axis, 0, 0)]
    psum x1 -> x0, blocking collectives: 7.63 us -> none  [local(): lax.psum((jnp.sum(node_out, -1), jnp.sum(node_out * node_out, -1)), 'sect')]
    gather x2 -> x0, local copies, waits for them, and re-layouts: 5.43 us -> none  [the longest x1 4.24 us: local(): halo = everything[flat_index]]
    all_gather x1 -> x2, blocking collectives: 16.2 us -> 11.8 us  [the longest x1 10 us: local(): offered_latent = lax.all_gather(offered_latent, 'sect', axis=1, tiled=True)]
    broadcast_in_dim x0 -> x4, local copies, waits for them, and re-layouts: none -> 3.99 us  [the longest x3 3.33 us: copies(): block = jnp.broadcast_to(block[None], (peers,) + block.shape)]
    dot_general x3 -> x8, matrix products: 6.44 us -> 10 us  [the longest x2 3.16 us: send(): jnp.dot(hidden, w2, preferred_element_type=jnp.float32) + b2]
  transfers between devices with their start and end apart: 1 -> 5, of which waited for: 1 -> 4; matrix products, arithmetic and copies ran while one was open for 2% -> 11% of each run, Pallas kernels for 0% -> 0%
where the time goes in v1:
time: 109 us; the launch traced here: 107 us
  starting transfers between devices  35 us (32%)
  blocking collectives  23.9 us (22%)
  waiting for transfers between devices  22.6 us (21%)
  matrix products  12.4 us (11%)
  local copies, waits for them, and re-layouts  9.02 us (8%)
  other arithmetic  3.55 us (3%)
    all_to_all x3, starting transfers between devices, copies(): return lax.all_to_all(block, axis, 0, 0)  20.7 us
    all_to_all x3, waiting for transfers between devices, copies(): return lax.all_to_all(block, axis, 0, 0)  12.2 us
    all_gather x1, blocking collectives, local(): whole_aggregate = lax.all_gather(aggregate, 'sect', axis=1, tiled=True)  12 us
    all_to_all x1, waiting for transfers between devices, local(): halo = lax.all_to_all(halo, 'y', 0, 0, tiled=True)  10.4 us
    all_gather x1, blocking collectives, local(): offered_latent = lax.all_gather(offered_latent, 'sect', axis=1, tiled=True)  10 us
    all_to_all x1, starting transfers between devices, local(): halo = lax.all_to_all(halo, 'y', 0, 0, tiled=True)  7.22 us
    all_to_all x1, starting transfers between devices, local(): lax.all_to_all(halo_slots.reshape(n_y, layer * takes), 'y', 0, 0, tiled=T...  7.1 us
    broadcast_in_dim x3, local copies, waits for them, and re-layouts, copies(): block = jnp.broadcast_to(block[None], (peers,) + block.shape)  3.33 us
  transfers between devices with their start and end apart: 5, of which 4 were waited for; matrix products, arithmetic and copies ran while one was open for 11% of the time, Pallas kernels for 0%

profile of v1, /device:TPU:6, one launch (start us, length us, event | category | flops | bytes accessed | tf_op | source)
XLA Modules:
  0.0 106.6 jit_solution(4220458792357003012)
XLA Ops:
  0.0 0.9 copy.17
  1.6 7.1 %all-to-all-start.1 = ((s32[8,1,128]{2,1,0:T(1,128)}), s32[8,1,128]{2,1,0:T(1,128)S(1)}, u32[]{:S(2)}, u32[]{:S(2)}) async-start(s32[8,1,128]{2,1,0:T(1,128)} %bitcast.4), calls=%async_computation.1 | async-start | bytes 8192 | tf_op jit(solution)/shard_map/all_to_all | solution.py:59
  8.7 1.1 %convolution_convert_fusion = bf16[32,128]{1,0:T(8,128)(2,1)S(1)} fusion(bf16[512,128]{1,0:T(8,128)(2,1)} %param.15, s32[32]{0:T(128)} %bitcast.55), kind=kOutput, calls=%fused_computation.22 | convolution fusion | flops 4214784 | bytes 139392 | tf_op jit(solution)/shard_map/dot_general | solution.py:20
  9.8 10.0 %all_gather.9 = bf16[32,512]{1,0:T(8,128)(2,1)S(1)} all-gather(bf16[32,128]{1,0:T(8,128)(2,1)S(1)} %convolution_convert_fusion), channel_id=1, replica_groups=mesh['y'=8,'z'=8,'core'=2,'sect'=4] {'sect'}, dimensions={1}, use_global_device_ids=true | all-gather | bytes 40960 | tf_op jit(solution)/shard_map/all_gather | solution.py:54
  19.9 1.4 %fusion.11 = bf16[32,128]{1,0:T(8,128)(2,1)S(1)} fusion(bf16[512,128]{1,0:T(8,128)(2,1)} %param.22, bf16[32,512]{1,0:T(8,128)(2,1)S(1)} %all_gather.9, bf16[512,512]{1,0:T(8,128)(2,1)} %param.20, f32[512]{0:T(512)} %param.21, f32[128]{0:T(128)} %param.23), kind=kOutput, calls=%fused_computation.21 | convolution fusion | flops 21078016 | bytes 698880 | tf_op jit(solution)/shard_map/dot_general | solution.py:14
  22.0 1.8 %all_gather.10 = bf16[64,128]{1,0:T(8,128)(2,1)S(1)} all-gather(bf16[32,128]{1,0:T(8,128)(2,1)S(1)} %fusion.11), channel_id=1, replica_groups=mesh['y'=8,'z'=8,'core'=2,'sect'=4] {'core'}, dimensions={0}, use_global_device_ids=true | all-gather | bytes 24576 | tf_op jit(solution)/shard_map/all_gather | solution.py:56
  24.5 10.3 %all-to-all-start.2 = ((bf16[8,64,128]{2,1,0:T(8,128)(2,1)}), bf16[8,64,128]{2,1,0:T(8,128)(2,1)S(1)}, u32[]{:S(2)}, u32[]{:S(2)}) async-start(bf16[8,64,128]{2,1,0:T(8,128)(2,1)} %broadcast_in_dim.11), calls=%async_computation.2 | async-start | bytes 262144 | tf_op jit(solution)/shard_map/all_to_all | solution.py:26
  34.9 1.2 %convert_element_type.54 = f32[128]{0:T(128)} convert(bf16[128]{0:T(256)(128)(2,1)} %param.27) | non-fusion elementwise | flops 128 | bytes 768 | tf_op jit(solution)/shard_map/convert_element_type | solution.py:96
  37.4 0.9 pad_maximum_fusion.3
  38.3 5.9 %all-to-all-done.2 = bf16[8,64,128]{2,1,0:T(8,128)(2,1)S(1)} async-done(((bf16[8,64,128]{2,1,0:T(8,128)(2,1)}), bf16[8,64,128]{2,1,0:T(8,128)(2,1)S(1)}, u32[]{:S(2)}, u32[]{:S(2)}) %all-to-all-start.2) | async-done | bytes 131104 | tf_op jit(solution)/shard_map/all_to_all | solution.py:26
  44.2 1.8 %broadcast_in_dim.10 = bf16[4,512,128]{2,1,0:T(8,128)(2,1)} broadcast(bf16[512,128]{1,0:T(8,128)(2,1)} %param.15), dimensions={1,2} | broadcast | bytes 655360 | tf_op jit(solution)/shard_map/broadcast_in_dim | solution.py:25
  46.0 4.9 %all-to-all-start = ((bf16[4,512,128]{2,1,0:T(8,128)(2,1)}), bf16[4,512,128]{2,1,0:T(8,128)(2,1)S(1)}, u32[]{:S(2)}, u32[]{:S(2)}) async-start(bf16[4,512,128]{2,1,0:T(8,128)(2,1)} %broadcast_in_dim.10), calls=%async_computation | async-start | bytes 1048576 | tf_op jit(solution)/shard_map/all_to_all | solution.py:26
  50.9 1.2 %fusion.2 = bf16[1024,128]{1,0:T(8,128)(2,1)} fusion(bf16[512,128]{1,0:T(8,128)(2,1)S(1)} %bitcast.52, s32[1024]{0:T(1024)S(1)} %bitcast_add_fusion), kind=kOutput, calls=%fused_computation.7 | convolution fusion | flops 134873088 | bytes 397312 | tf_op jit(solution)/shard_map/dot_general | solution.py:20
  52.1 5.1 %all-to-all-done = bf16[4,512,128]{2,1,0:T(8,128)(2,1)S(1)} async-done(((bf16[4,512,128]{2,1,0:T(8,128)(2,1)}), bf16[4,512,128]{2,1,0:T(8,128)(2,1)S(1)}, u32[]{:S(2)}, u32[]{:S(2)}) %all-to-all-start) | async-done | bytes 524320 | tf_op jit(solution)/shard_map/all_to_all | solution.py:26
  58.1 5.5 %all-to-all-start.4 = ((bf16[4,528,128]{2,1,0:T(8,128)(2,1)}), bf16[4,528,128]{2,1,0:T(8,128)(2,1)S(1)}, u32[]{:S(2)}, u32[]{:S(2)}) async-start(bf16[4,528,128]{2,1,0:T(8,128)(2,1)} %broadcast_in_dim.14), calls=%async_computation.4 | async-start | bytes 1081344 | tf_op jit(solution)/shard_map/all_to_all | solution.py:26
  64.3 2.4 %fusion.17 = f32[512,512]{1,0:T(8,128)} fusion(bf16[1024,512]{1,0:T(8,128)(2,1)} %param.24, bf16[512,128]{1,0:T(8,128)(2,1)S(1)} %get-tuple-element.12, bf16[512,128]{1,0:T(8,128)(2,1)S(1)} %get-tuple-element.13, bf16[512,128]{1,0:T(8,128)(2,1)S(1)} %get-tuple-element.14, bf16[512,128]{1,0:T(8,128)(2,1)S(1)} %get-tuple-element.11), kind=kOutput, calls=%fused_computation.33 | convolution fusion | flops 270532608 | bytes 2097152 | tf_op jit(solution)/shard_map/dot_general | solution.py:84
  66.8 1.7 %fusion.8 = bf16[512,128]{1,0:T(8,128)(2,1)S(1)} fusion(bf16[512,128]{1,0:T(8,128)(2,1)} %param.22, bf16[512,512]{1,0:T(8,128)(2,1)S(1)} %copy-done.7, f32[512]{0:T(512)} %param.21, f32[128]{0:T(128)} %param.23, bf16[512,128]{1,0:T(8,128)(2,1)S(1)} %get-tuple-element.12, bf16[512,128]{1,0:T(8,128)(2,1)} %copy-done.3, bf16[512,128]{1,0:T(8,128)(2,1)} %copy-done.4, ...), kind=kOutput, calls=%fused_computation.16 | convolution fusion | flops 339345408 | bytes 1313280 | tf_op jit(solution)/shard_map/dot_general | solution.py:14
  68.5 1.2 %all-to-all-done.4 = bf16[4,528,128]{2,1,0:T(8,128)(2,1)S(1)} async-done(((bf16[4,528,128]{2,1,0:T(8,128)(2,1)}), bf16[4,528,128]{2,1,0:T(8,128)(2,1)S(1)}, u32[]{:S(2)}, u32[]{:S(2)}) %all-to-all-start.4) | async-done | bytes 540704 | tf_op jit(solution)/shard_map/all_to_all | solution.py:26
  69.7 7.2 %all-to-all-start.3 = ((bf16[8,128,128]{2,1,0:T(8,128)(2,1)}), bf16[8,128,128]{2,1,0:T(8,128)(2,1)S(1)}, u32[]{:S(2)}, u32[]{:S(2)}) async-start(bf16[8,128,128]{2,1,0:T(8,128)(2,1)} %bitcast.9), calls=%async_computation.3 | async-start | bytes 524288 | tf_op jit(solution)/shard_map/all_to_all | solution.py:62
  77.0 10.4 %all-to-all-done.3 = bf16[8,128,128]{2,1,0:T(8,128)(2,1)S(1)} async-done(((bf16[8,128,128]{2,1,0:T(8,128)(2,1)}), bf16[8,128,128]{2,1,0:T(8,128)(2,1)S(1)}, u32[]{:S(2)}, u32[]{:S(2)}) %all-to-all-start.3) | async-done | bytes 262176 | tf_op jit(solution)/shard_map/all_to_all | solution.py:62
  87.4 2.1 %gather_fusion = bf16[64,128,128]{2,1,0:T(8,128)(2,1)} fusion(bf16[12,128,128]{2,1,0:T(8,128)(2,1)S(1)} %bitcast.48, s32[1024]{0:T(1024)S(1)} %copy-done.5), kind=kCustom, calls=%fused_computation | custom fusion | bytes 4194560 | tf_op jit(solution)/shard_map/gather | solution.py:79
  89.6 2.4 %fusion.10 = bf16[4,128,128]{1,2,0:T(8,128)(2,1)S(1)} fusion(bf16[4,16,128,128]{3,2,1,0:T(8,128)(2,1)S(1)} %copy-done, bf16[4,16,128,128]{3,2,1,0:T(8,128)(2,1)} %bitcast.49), kind=kOutput, calls=%fused_computation.18 | convolution fusion | flops 268500992 | bytes 4325376 | tf_op jit(solution)/shard_map/bkij,bkjc->bic/dot_general | solution.py:80
  92.0 12.0 %all_gather.11 = bf16[512,512]{1,0:T(8,128)(2,1)S(1)} all-gather(bf16[512,128]{1,0:T(8,128)(2,1)S(1)} %bitcast.51), channel_id=1, replica_groups=mesh['y'=8,'z'=8,'core'=2,'sect'=4] {'sect'}, dimensions={1}, use_global_device_ids=true | all-gather | bytes 655360 | tf_op jit(solution)/shard_map/all_gather | solution.py:82
  105.6 1.0 fusion.9
  (44 shorter events, 6.7 us)
Async XLA Ops:
  0.0 89.6 %copy-start = (bf16[4,16,128,128]{3,2,1,0:T(8,128)(2,1)S(1)}, bf16[4,16,128,128]{3,2,1,0:T(8,128)(2,1)}, u32[]{:S(2)}) copy-start(bf16[4,16,128,128]{3,2,1,0:T(8,128)(2,1)} %param.19) | copy-start | bytes 6291460
  1.6 22.2 %all-to-all-start.1 = ((s32[8,1,128]{2,1,0:T(1,128)}), s32[8,1,128]{2,1,0:T(1,128)S(1)}, u32[]{:S(2)}, u32[]{:S(2)}) async-start(s32[8,1,128]{2,1,0:T(1,128)} %bitcast.4), calls=%async_computation.1 | async-start | bytes 8192 | tf_op jit(solution)/shard_map/all_to_all | solution.py:59
  24.5 19.7 %all-to-all-start.2 = ((bf16[8,64,128]{2,1,0:T(8,128)(2,1)}), bf16[8,64,128]{2,1,0:T(8,128)(2,1)S(1)}, u32[]{:S(2)}, u32[]{:S(2)}) async-start(bf16[8,64,128]{2,1,0:T(8,128)(2,1)} %broadcast_in_dim.11), calls=%async_computation.2 | async-start | bytes 262144 | tf_op jit(solution)/shard_map/all_to_all | solution.py:26
  46.0 11.2 %all-to-all-start = ((bf16[4,512,128]{2,1,0:T(8,128)(2,1)}), bf16[4,512,128]{2,1,0:T(8,128)(2,1)S(1)}, u32[]{:S(2)}, u32[]{:S(2)}) async-start(bf16[4,512,128]{2,1,0:T(8,128)(2,1)} %broadcast_in_dim.10), calls=%async_computation | async-start | bytes 1048576 | tf_op jit(solution)/shard_map/all_to_all | solution.py:26
  58.1 11.6 %all-to-all-start.4 = ((bf16[4,528,128]{2,1,0:T(8,128)(2,1)}), bf16[4,528,128]{2,1,0:T(8,128)(2,1)S(1)}, u32[]{:S(2)}, u32[]{:S(2)}) async-start(bf16[4,528,128]{2,1,0:T(8,128)(2,1)} %broadcast_in_dim.14), calls=%async_computation.4 | async-start | bytes 1081344 | tf_op jit(solution)/shard_map/all_to_all | solution.py:26
  63.6 0.7 copy-start.3
  63.6 0.7 copy-start.4
  63.6 3.1 %copy-start.7 = (bf16[512,512]{1,0:T(8,128)(2,1)S(1)}, bf16[512,512]{1,0:T(8,128)(2,1)}, u32[]{:S(2)}) copy-start(bf16[512,512]{1,0:T(8,128)(2,1)} %param.20) | copy-start | bytes 1572868
  68.5 18.9 %copy-start.5 = (s32[1024]{0:T(1024)S(1)}, s32[1024]{0:T(1024)}, u32[]{:S(2)}) copy-start(s32[1024]{0:T(1024)} %pad_clamp_fusion) | copy-start | bytes 12292
  69.7 17.7 %all-to-all-start.3 = ((bf16[8,128,128]{2,1,0:T(8,128)(2,1)}), bf16[8,128,128]{2,1,0:T(8,128)(2,1)S(1)}, u32[]{:S(2)}, u32[]{:S(2)}) async-start(bf16[8,128,128]{2,1,0:T(8,128)(2,1)} %bitcast.9), calls=%async_computation.3 | async-start | bytes 524288 | tf_op jit(solution)/shard_map/all_to_all | solution.py:62
  89.6 14.5 %copy-start.6 = (bf16[1024,512]{1,0:T(8,128)(2,1)S(1)}, bf16[1024,512]{1,0:T(8,128)(2,1)}, u32[]{:S(2)}) copy-start(bf16[1024,512]{1,0:T(8,128)(2,1)} %param.24) | copy-start | bytes 3145732
  89.6 14.5 %copy-start.8 = (f32[512]{0:T(512)S(1)}, f32[512]{0:T(512)}, u32[]{:S(2)}) copy-start(f32[512]{0:T(512)} %param.25) | copy-start | bytes 6148
  89.6 14.5 %copy-start.12 = (f32[512,512]{1,0:T(8,128)S(1)}, f32[512,512]{1,0:T(8,128)}, u32[]{:S(2)}) copy-start(f32[512,512]{1,0:T(8,128)} %fusion.17) | copy-start | bytes 3145732
  104.7 0.9 copy-start.1
  104.7 1.0 copy-start.2
  104.7 1.0 copy-start.9
  104.7 0.9 copy-start.10
  104.7 0.9 copy-start.11

commit v2 on v1

v2 whole, which is shorter than its diff:
```python
import jax
import jax.numpy as jnp
from jax import lax
from jax.experimental import pallas as pl
from jax.experimental.pallas import tpu as pltpu
from jax.sharding import Mesh
from jax.sharding import PartitionSpec as P

NODE = ("y", "z", "core")
EPS = 1e-05
TAIL = 16

LIMIT = 60 << 20
WEIGHT = 10**10
bf16, f32, i32 = jnp.bfloat16, jnp.float32, jnp.int32


def call(body, operands, outs, scratch=(), scalars=(), part={}, flops=0, moved=0):
    count = len(operands)
    space = [pltpu.SMEM if i in scalars else pltpu.VMEM for i in range(count)]

    def kernel(*refs):
        sources, rest = refs[:count], refs[count:]
        results, held, rest = rest[: len(outs)], rest[len(outs) :][:count], rest[len(outs) + count :]
        sems, extra = rest[-1], rest[:-1]
        copies = [
            pltpu.make_async_copy(
                source.at[pl.ds(*part[i])] if i in part else source, target, sems.at[i]
            )
            for i, (source, target) in enumerate(zip(sources, held))
        ]
        for copy in copies:
            copy.start()

        def ready(i):
            def get():
                if copies[i] is not None:
                    copies[i].wait()
                    copies[i] = None
                return held[i]

            return get

        gets = [ready(i) for i in range(count)]
        body(*gets, *results, *extra)
        for get in gets:
            get()

    return pl.pallas_call(
        kernel,
        out_shape=[jax.ShapeDtypeStruct(shape, kind) for shape, kind in outs],
        in_specs=[pl.BlockSpec(memory_space=pltpu.HBM)] * count,
        out_specs=[pl.BlockSpec(memory_space=pltpu.VMEM)] * len(outs),
        scratch_shapes=[
            kind((part[i][1],) + v.shape[1:] if i in part else v.shape, v.dtype)
            for i, (kind, v) in enumerate(zip(space, operands))
        ]
        + list(scratch)
        + [pltpu.SemaphoreType.DMA((count,))],
        compiler_params=pltpu.CompilerParams(vmem_limit_bytes=LIMIT),
        cost_estimate=pl.CostEstimate(flops=flops, bytes_accessed=moved, transcendentals=0),
        name=body.__name__,
    )(*operands)


def matmul(left, right):
    return jnp.dot(left, right, preferred_element_type=f32)


def silu(value):
    half = 0.5 * value
    return half + half * jnp.tanh(half)


def pack(export, latent, slots, offered, wanted, wide):
    rows, offers = latent().shape[0], offered.shape[0]
    wide[pl.ds(0, rows), :] = latent()[...].astype(f32)
    chosen = export()
    for e in range(offers):
        wide[pl.ds(rows + e, 1), :] = wide[pl.ds(chosen[0, e], 1), :]
    offered[...] = wide[pl.ds(rows, offers), :].astype(bf16)
    for peer in range(wanted.shape[0]):
        wanted[peer] = slots()[...]


def offer(gathered, w1, b1, w2, b2, out):
    offers = out.shape[1]
    parts = gathered().shape[0] // offers
    rows = jnp.concatenate([gathered()[pl.ds(p * offers, offers), :] for p in range(parts)], 1)
    hidden = silu(matmul(rows, w1()[...]) + b1()[...]).astype(bf16)
    message = (matmul(hidden, w2()[...]) + b2()[...]).astype(bf16)
    for peer in range(out.shape[0]):
        out[peer] = message


def bundle(latent, w2, b2, side):
    rows = latent().shape[0]
    side[pl.ds(0, rows), :] = latent()[...]
    side[pl.ds(rows, rows), :] = w2()[...]
    row = b2()[...].astype(f32)
    side[pl.ds(2 * rows, TAIL), :] = jnp.broadcast_to(row, (TAIL, row.shape[1])).astype(bf16)


def select(wanted, offered, out):
    wanted, offered = wanted(), offered()
    n_y, takes, lanes = wanted.shape
    layer = lanes // n_y
    n_z = layer // 2
    offers = offered.shape[0] // layer
    quad = 128 // offers
    half = offered.shape[0] // 2
    shift = lax.rem(lanes - lax.axis_index("y") * layer, lanes)
    lane = lax.broadcasted_iota(i32, (takes, 128), 1)
    blank = jnp.zeros((takes, 128), f32)
    for q in range(n_z // quad):
        sources = jnp.concatenate(
            [offered[pl.ds(c * half + q * 128, 128), :] for c in range(2)], 0
        )
        chosen = []
        for peer in range(n_y):
            table = pltpu.roll(wanted[peer], shift, 1)
            for part in range(quad):
                z = q * quad + part
                first, second = [
                    jnp.where(
                        table[:, 2 * z + c : 2 * z + c + 1] + part * offers == lane, 1.0, 0.0
                    )
                    for c in range(2)
                ]
                chosen.append(jnp.concatenate([first, blank], 1))
                chosen.append(jnp.concatenate([blank, second], 1))
        chosen = jnp.concatenate(chosen, 0).astype(bf16)
        rows = matmul(chosen, sources).astype(bf16)
        depth = quad * 2 * takes
        for peer in range(n_y):
            out[peer, pl.ds(q * depth, depth), :] = rows[peer * depth : (peer + 1) * depth]


def send(side0, side1, side2, side3, w1, b1, w2, b2, upper_w, message, upper):
    rows, share = message.shape
    width = upper.shape[1]
    sides = [side() for side in (side0, side1, side2, side3)]
    parts = len(sides)
    here = lax.axis_index("sect")
    order = [lax.rem(here + parts - k, parts) * share for k in range(parts)]

    def rolled(values):
        return jnp.concatenate([values[pl.ds(pl.multiple_of(o, share), share), :] for o in order], 0)

    step = rows // 2
    for turn in range(2):
        now = rolled(w1() if turn == 0 else upper_w())
        for r in range(0, rows, step):
            at = pl.ds(r, step)
            x = jnp.concatenate([side[at, :] for side in sides], 1)
            if turn == 0:
                hidden = silu(matmul(x, now) + b1()[...]).astype(bf16)
                message[at, :] = (matmul(hidden, w2()[...]) + b2()[...]).astype(bf16)
            else:
                upper[at, :] = matmul(x, now)


def tiles(source, message, halo, weight, out, extended):
    tile, share = extended.shape[1:]
    own = message().shape[0] // tile
    for b in range(own):
        extended[b] = message()[pl.ds(b * tile, tile), :]
    for b in range(halo().shape[0]):
        extended[own + b] = halo()[b]
    src = source()
    blocks, terms = src.shape
    group = 4
    for b in range(blocks):
        total = jnp.zeros((tile, share), f32)
        for k in range(0, terms, group):
            left = jnp.concatenate([weight()[b, k + g] for g in range(group)], 1)
            right = jnp.concatenate([extended[src[b, k + g]] for g in range(group)], 0)
            total = total + matmul(left, right)
        total = total.astype(bf16)
        for peer in range(out.shape[0]):
            out[peer, pl.ds(b * tile, tile), :] = total


def node(aggregate, lower_w, upper, b1, side0, side1, side2, side3, gain, bias, out):
    parts, rows, share = aggregate().shape
    sides = [side() for side in (side0, side1, side2, side3)]
    w2 = jnp.concatenate([side[pl.ds(rows, rows), :] for side in sides], 1)
    b2 = jnp.concatenate([side[pl.ds(2 * rows, 1), :] for side in sides], 1).astype(f32)
    width = share * parts
    step = rows // 2
    for r in range(0, rows, step):
        at = pl.ds(r, step)
        x = jnp.concatenate([aggregate()[p, at, :] for p in range(parts)], 1)
        hidden = silu(upper()[at, :] + matmul(x, lower_w()[...]) + b1()[...]).astype(bf16)
        every = matmul(hidden, w2) + b2
        split = [every[:, p * share : (p + 1) * share] for p in range(parts)]
        mine = split[0]
        total = jnp.sum(sum(split), 1, keepdims=True)
        squares = jnp.sum(sum(v * v for v in split), 1, keepdims=True)
        mean = total * (1.0 / width)
        var = squares * (1.0 / width) - mean * mean
        normed = (mine - mean) * lax.rsqrt(var + EPS)
        latent = sides[0][at, :].astype(f32)
        out[at, :] = (latent + gain()[...] * normed + bias()[...]).astype(bf16)


def local(
    latent,
    export_rows,
    halo_slots,
    tile_src,
    tile_weight,
    send_w1,
    send_b1,
    send_w2,
    send_b2,
    node_w1,
    node_b1,
    node_w2,
    node_b2,
    ln_gain,
    ln_bias,
):
    rows, share = latent.shape
    width = send_w1.shape[0]
    offers = export_rows.shape[1]
    takes = halo_slots.shape[2]
    n_y, n_z, n_core, n_sect = (lax.axis_size(name) for name in NODE + ("sect",))
    layer = n_z * n_core
    tile = tile_weight.shape[-1]
    send_b1, send_b2, node_b1, node_b2, ln_gain, ln_bias = (
        v[None] for v in (send_b1, send_b2, node_b1, node_b2, ln_gain, ln_bias)
    )

    sender = (send_w1, send_b1, send_w2, send_b2)
    slots = jnp.swapaxes(halo_slots[0], 0, 1)
    offered, wanted = call(
        pack,
        (export_rows, latent, slots),
        [((offers, share), bf16), ((n_y, takes, n_y * layer), i32)],
        [pltpu.VMEM((rows + offers, share), f32)],
        scalars=(0,),
    )

    wanted = lax.all_to_all(wanted, "y", 0, 0)
    for pairs in ([[0, 1], [2, 3]], [[0, 3], [1, 2]]):
        offered = lax.all_gather(offered, "sect", axis=0, tiled=True, axis_index_groups=pairs)
    offered, wanted = lax.optimization_barrier((offered, wanted))
    (offered,) = call(offer, (offered, *sender), [((n_z, offers, share), bf16)])

    offered, latent, node_w2, node_b2 = lax.optimization_barrier(
        (offered, latent, node_w2, node_b2)
    )
    offered = lax.all_to_all(offered, "z", 0, 0).reshape(n_z * offers, share)
    (side,) = call(
        bundle,
        (latent, node_w2, node_b2),
        [((2 * rows + TAIL, share), bf16)],
        flops=WEIGHT,
        moved=4 * rows * share,
    )
    sides = [side] + [
        lax.ppermute(side, "sect", [(i, (i + k) % n_sect) for i in range(n_sect)])
        for k in range(1, n_sect)
    ]
    offered = lax.all_gather(offered, "core", axis=0, tiled=True)
    (halo,) = call(
        select,
        (wanted, offered),
        [((n_y, layer * takes, share), bf16)],
        flops=2 * WEIGHT,
    )

    halo, *sides = lax.optimization_barrier((halo, *sides))
    halo = lax.all_to_all(halo, "y", 0, 0)
    message, upper = call(
        send,
        (*sides, *sender, node_w1),
        [((rows, share), bf16), ((rows, width), f32)],
        part={8: (0, width)},
        flops=2 * rows * width * (2 * width + share),
        moved=4 * rows * width,
    )

    (aggregate,) = call(
        tiles,
        (tile_src, message, halo, tile_weight),
        [((n_sect, rows, share), bf16)],
        [pltpu.VMEM((rows // tile + n_y, tile, share), bf16)],
        scalars=(0,),
    )
    aggregate = lax.all_to_all(aggregate, "sect", 0, 0)

    (updated,) = call(
        node,
        (aggregate, node_w1, upper, node_b1, *sides, ln_gain, ln_bias),
        [((rows, share), bf16)],
        part={1: (width, width)},
    )
    return updated


def solution(mesh):
    n_mesh, n_sect = mesh.devices.shape
    n_y = n_z = int(round((n_mesh // 2) ** 0.5))
    grid = Mesh(mesh.devices.reshape(n_y, n_z, 2, n_sect), NODE + ("sect",))
    in_specs = (
        P(NODE, "sect"),
        P(NODE, None),
        P(NODE, None, None),
        P(NODE, None),
        P(NODE, None, None, None),
        P(),
        P(),
        P(None, "sect"),
        P("sect"),
        P(),
        P(),
        P(None, "sect"),
        P("sect"),
        P("sect"),
        P("sect"),
    )
    out_specs = P(NODE, "sect")
    return jax.shard_map(local, mesh=grid, in_specs=in_specs, out_specs=out_specs, check_vma=False)
```

time: 109 us -> 90.2 us (0.83)
  Pallas kernels: 0 us -> 18.9 us
  matrix products: 12.4 us -> 0 us
  waiting for transfers between devices: 22.6 us -> 10.4 us
  local copies, waits for them, and re-layouts: 9.02 us -> 0.73 us
  other arithmetic: 3.55 us -> 0 us
  starting transfers between devices: 35 us -> 33.2 us
  blocking collectives: 23.9 us -> 25.2 us
    pallas_call x0 -> x7, Pallas kernels: none -> 18.9 us  [call(): pl.pallas_call(kernel, out_shape=[jax.ShapeDtypeStruct(shape, kind) for s...]
    all_to_all x5 -> x3, waiting for transfers between devices: 22.6 us -> 6.62 us  [the longest x1 6.62 us: local(): halo = lax.all_to_all(halo, 'y', 0, 0)]
    all_to_all x0 -> x1, blocking collectives: none -> 12.8 us  [local(): aggregate = lax.all_to_all(aggregate, 'sect', 0, 0)]
    dot_general x9 -> x0, matrix products: 12.4 us -> none  [the longest x2 3.16 us: send(): jnp.dot(hidden, w2, preferred_element_type=jnp.float32) + b2]
    all_gather x2, blocking collectives: 22.1 us -> 10.3 us  [local(): lax.all_gather(offered, 'sect', axis=0, tiled=True, axis_index_groups=pairs)]
    all_to_all x5 -> x3, starting transfers between devices: 35 us -> 24.2 us  [the longest x1 10.3 us: local(): offered = lax.all_to_all(offered, 'z', 0, 0).reshape(n_z * offers, share)]
    ppermute x0 -> x3, starting transfers between devices: none -> 8.97 us  [local(): lax.ppermute(side, 'sect', [(i, (i + k) % n_sect) for i in range(n_sect)])]
    broadcast_in_dim x5 -> x0, local copies, waits for them, and re-layouts: 4.07 us -> none  [the longest x3 3.33 us: copies(): block = jnp.broadcast_to(block[None], (peers,) + block.shape)]
  transfers between devices with their start and end apart: 5 -> 6, of which waited for: 4 -> 3; matrix products, arithmetic and copies ran while one was open for 11% -> 0% of each run, Pallas kernels for 0% -> 4%
where the time goes in v2:
time: 90.2 us; the launch traced here: 88.5 us
  starting transfers between devices  33.2 us (37%)
  blocking collectives  25.2 us (28%)
  Pallas kernels  18.9 us (21%)
  waiting for transfers between devices  10.4 us (12%)
    pallas_call x7, Pallas kernels, call(): pl.pallas_call(kernel, out_shape=[jax.ShapeDtypeStruct(shape, kind) for s...  18.9 us
    all_to_all x1, blocking collectives, local(): aggregate = lax.all_to_all(aggregate, 'sect', 0, 0)  12.8 us
    all_to_all x1, starting transfers between devices, local(): offered = lax.all_to_all(offered, 'z', 0, 0).reshape(n_z * offers, share)  10.3 us
    all_gather x2, blocking collectives, local(): lax.all_gather(offered, 'sect', axis=0, tiled=True, axis_index_groups=pairs)  10.3 us
    ppermute x3, starting transfers between devices, local(): lax.ppermute(side, 'sect', [(i, (i + k) % n_sect) for i in range(n_sect)])  8.97 us
    all_to_all x1, starting transfers between devices, local(): wanted = lax.all_to_all(wanted, 'y', 0, 0)  7.11 us
    all_to_all x1, starting transfers between devices, local(): halo = lax.all_to_all(halo, 'y', 0, 0)  6.8 us
    all_to_all x1, waiting for transfers between devices, local(): halo = lax.all_to_all(halo, 'y', 0, 0)  6.62 us
  transfers between devices with their start and end apart: 6, of which 3 were waited for; matrix products, arithmetic and copies ran while one was open for 0% of the time, Pallas kernels for 4%

profile of v2, /device:TPU:6, one launch (start us, length us, event | category | flops | bytes accessed | tf_op | source)
XLA Modules:
  0.0 88.5 jit_solution(2380600626349149146)
XLA Ops:
  0.0 1.7 %pack.1 = (bf16[32,128]{1,0:T(8,128)(2,1)}, s32[8,8,128]{2,1,0:T(8,128)}) custom-call(s32[1,32]{1,0:T(1,128)} %refs_0_.2, bf16[512,128]{1,0:T(8,128)(2,1)} %refs_0_.3, s32[8,128]{1,0:T(8,128)} %bitcast.13), custom_call_target="tpu_custom_call" | custom-call | tf_op jit(solution)/shard_map/pack/pallas_call | solution.py:49
  1.7 7.1 %all-to-all-start = ((s32[8,8,128]{2,1,0:T(8,128)}), s32[8,8,128]{2,1,0:T(8,128)S(1)}, u32[]{:S(2)}, u32[]{:S(2)}) async-start(s32[8,8,128]{2,1,0:T(8,128)} %get-tuple-element.21), calls=%async_computation | async-start | bytes 65536 | tf_op jit(solution)/shard_map/all_to_all | solution.py:245
  8.8 4.6 %all_gather.9 = bf16[64,128]{1,0:T(8,128)(2,1)S(1)} all-gather(bf16[32,128]{1,0:T(8,128)(2,1)} %get-tuple-element.20), channel_id=1, replica_groups={{0,1},{2,3},{4,5},{6,7},{8,9},{10,11},{12,13},{14,15},{16,17},{18,19},{..., dimensions={0}, use_global_device_ids=true | all-gather | bytes 24576 | tf_op jit(solution)/shard_map/all_gather | solution.py:247
  13.4 5.7 %all_gather.10.refs_0_ = bf16[128,128]{1,0:T(8,128)(2,1)} all-gather(bf16[64,128]{1,0:T(8,128)(2,1)S(1)} %all_gather.9), channel_id=1, replica_groups={{0,3},{1,2},{4,7},{5,6},{8,11},{9,10},{12,15},{13,14},{16,19},{17,18},{..., dimensions={0}, use_global_device_ids=true | all-gather | bytes 49152 | tf_op jit(solution)/shard_map/all_gather | solution.py:247
  19.1 0.0 all-to-all-done.refs_0_
  19.1 2.1 %offer.1 = bf16[8,32,128]{2,1,0:T(8,128)(2,1)} custom-call(bf16[128,128]{1,0:T(8,128)(2,1)} %all_gather.10.refs_0_, bf16[512,512]{1,0:T(8,128)(2,1)} %refs_4_.1, f32[1,512]{1,0:T(1,128)} %bitcast.11, bf16[512,128]{1,0:T(8,128)(2,1)} %refs_6_.1, f32[1,128]{1,0:T(1,128)} %bitcast.15), custom_call_target="tpu_custom_call" | custom-call | tf_op jit(solution)/shard_map/offer/pallas_call | solution.py:49
  21.2 10.3 %all-to-all-start.1 = ((bf16[8,32,128]{2,1,0:T(8,128)(2,1)}), bf16[8,32,128]{2,1,0:T(8,128)(2,1)S(1)}, u32[]{:S(2)}, u32[]{:S(2)}) async-start(bf16[8,32,128]{2,1,0:T(8,128)(2,1)} %offer.1), calls=%async_computation.1 | async-start | bytes 131072 | tf_op jit(solution)/shard_map/all_to_all | solution.py:254
  31.6 1.7 %bundle.1.refs_0_.refs_4_ = bf16[1040,128]{1,0:T(8,128)(2,1)} custom-call(bf16[512,128]{1,0:T(8,128)(2,1)} %refs_0_.3, bf16[512,128]{1,0:T(8,128)(2,1)} %refs_1_.5, bf16[1,128]{1,0:T(2,128)(2,1)} %bitcast.19), custom_call_target="tpu_custom_call" | custom-call | flops 10000000000 | bytes 262144 | tf_op jit(solution)/shard_map/bundle/pallas_call | solution.py:49
  33.3 1.9 %collective-permute-start.2 = (bf16[1040,128]{1,0:T(8,128)(2,1)}, bf16[1040,128]{1,0:T(8,128)(2,1)S(1)}, u32[]{:S(2)}, u32[]{:S(2)}) collective-permute-start(bf16[1040,128]{1,0:T(8,128)(2,1)} %bundle.1.refs_0_.refs_4_), channel_id=1, source_target_pairs={{0,3},{1,0},{2,1},{3,2},{4,7},{5,4},{6,5},{7,6},{8,11},{9,8},{10,9... | collective-permute-start | bytes 798728 | tf_op jit(solution)/shard_map/ppermute | solution.py:263
  35.2 3.8 %collective-permute-start.1 = (bf16[1040,128]{1,0:T(8,128)(2,1)}, bf16[1040,128]{1,0:T(8,128)(2,1)S(1)}, u32[]{:S(2)}, u32[]{:S(2)}) collective-permute-start(bf16[1040,128]{1,0:T(8,128)(2,1)} %bundle.1.refs_0_.refs_4_), channel_id=1, source_target_pairs={{0,2},{1,3},{2,0},{3,1},{4,6},{5,7},{6,4},{7,5},{8,10},{9,11},{10,... | collective-permute-start | bytes 798728 | tf_op jit(solution)/shard_map/ppermute | solution.py:263
  39.1 3.2 %collective-permute-start = (bf16[1040,128]{1,0:T(8,128)(2,1)}, bf16[1040,128]{1,0:T(8,128)(2,1)S(1)}, u32[]{:S(2)}, u32[]{:S(2)}) collective-permute-start(bf16[1040,128]{1,0:T(8,128)(2,1)} %bundle.1.refs_0_.refs_4_), channel_id=1, source_target_pairs={{0,1},{1,2},{2,3},{3,0},{4,5},{5,6},{6,7},{7,4},{8,9},{9,10},{10,1... | collective-permute-start | bytes 798728 | tf_op jit(solution)/shard_map/ppermute | solution.py:263
  42.3 0.0 all-to-all-done.1
  42.3 2.0 %all_gather.11.refs_1_ = bf16[512,128]{1,0:T(8,128)(2,1)} all-gather(bf16[256,128]{1,0:T(8,128)(2,1)S(1)} %bitcast.10), channel_id=1, replica_groups=mesh['y'=8,'z'=8,'core'=2,'sect'=4] {'core'}, dimensions={0}, use_global_device_ids=true | all-gather | bytes 196608 | tf_op jit(solution)/shard_map/all_gather | solution.py:266
  44.3 2.2 %select.1 = bf16[8,128,128]{2,1,0:T(8,128)(2,1)} custom-call(s32[8,8,128]{2,1,0:T(8,128)} %copy-done.4, bf16[512,128]{1,0:T(8,128)(2,1)} %all_gather.11.refs_1_), custom_call_target="tpu_custom_call" | custom-call | flops 20000000000 | tf_op jit(solution)/shard_map/select/pallas_call | solution.py:49
  46.5 1.3 %collective-permute-done.2.refs_3_.refs_7_ = bf16[1040,128]{1,0:T(8,128)(2,1)S(1)} collective-permute-done((bf16[1040,128]{1,0:T(8,128)(2,1)}, bf16[1040,128]{1,0:T(8,128)(2,1)S(1)}, u32[]{:S(2)}, u32[]{:S(2)}) %collective-permute-start.2) | collective-permute-done | bytes 266272 | tf_op jit(solution)/shard_map/ppermute | solution.py:263
  47.8 0.0 collective-permute-done.1.refs_2_.refs_6_
  47.8 2.5 %collective-permute-done.refs_1_.refs_5_ = bf16[1040,128]{1,0:T(8,128)(2,1)S(1)} collective-permute-done((bf16[1040,128]{1,0:T(8,128)(2,1)}, bf16[1040,128]{1,0:T(8,128)(2,1)S(1)}, u32[]{:S(2)}, u32[]{:S(2)}) %collective-permute-start) | collective-permute-done | bytes 266272 | tf_op jit(solution)/shard_map/ppermute | solution.py:263
  50.3 6.8 %all-to-all-start.2 = ((bf16[8,128,128]{2,1,0:T(8,128)(2,1)}), bf16[8,128,128]{2,1,0:T(8,128)(2,1)S(1)}, u32[]{:S(2)}, u32[]{:S(2)}) async-start(bf16[8,128,128]{2,1,0:T(8,128)(2,1)} %select.1), calls=%async_computation.2 | async-start | bytes 524288 | tf_op jit(solution)/shard_map/all_to_all | solution.py:275
  57.1 3.8 %send.1 = (bf16[512,128]{1,0:T(8,128)(2,1)}, f32[512,512]{1,0:T(8,128)}) custom-call(bf16[1040,128]{1,0:T(8,128)(2,1)} %bundle.1.refs_0_.refs_4_, bf16[1040,128]{1,0:T(8,128)(2,1)} %copy-done.2, bf16[1040,128]{1,0:T(8,128)(2,1)} %copy-done.1, bf16[1040,128]{1,0:T(8,128)(2,1)} %copy-done, bf16[512,512]{1,0:T(8,128)(2,1)} %refs_4_.1, f32[1,512]{1,0:T(1,128)} %bitcast.12, ...), custom_call_target="tpu_custom_call" | custom-call | flops 603979776 | bytes 1048576 | tf_op jit(solution)/shard_map/send/pallas_call | solution.py:49
  61.0 6.6 %all-to-all-done.2.refs_2_ = bf16[8,128,128]{2,1,0:T(8,128)(2,1)S(1)} async-done(((bf16[8,128,128]{2,1,0:T(8,128)(2,1)}), bf16[8,128,128]{2,1,0:T(8,128)(2,1)S(1)}, u32[]{:S(2)}, u32[]{:S(2)}) %all-to-all-start.2) | async-done | bytes 262176 | tf_op jit(solution)/shard_map/all_to_all | solution.py:275
  67.6 0.7 copy-done.3
  68.3 3.3 %tiles.1 = bf16[4,512,128]{2,1,0:T(8,128)(2,1)} custom-call(s32[4,16]{1,0:T(4,128)} %refs_0_.4, bf16[512,128]{1,0:T(8,128)(2,1)} %get-tuple-element.32.refs_1_, bf16[8,128,128]{2,1,0:T(8,128)(2,1)} %copy-done.3, bf16[4,16,128,128]{3,2,1,0:T(8,128)(2,1)} %refs_3_.3), custom_call_target="tpu_custom_call" | custom-call | tf_op jit(solution)/shard_map/tiles/pallas_call | solution.py:49
  71.6 12.8 %all_to_all.20.refs_0_ = bf16[4,512,128]{2,1,0:T(8,128)(2,1)} all-to-all(bf16[4,512,128]{2,1,0:T(8,128)(2,1)} %tiles.1), channel_id=1, replica_groups=mesh['y'=8,'z'=8,'core'=2,'sect'=4] {'sect'}, dimensions={0} | all-to-all | bytes 1048576 | tf_op jit(solution)/shard_map/all_to_all | solution.py:292
  84.5 4.1 %node.1 = bf16[512,128]{1,0:T(8,128)(2,1)} custom-call(bf16[4,512,128]{2,1,0:T(8,128)(2,1)} %all_to_all.20.refs_0_, bf16[1024,512]{1,0:T(8,128)(2,1)} %refs_1_.6, f32[512,512]{1,0:T(8,128)} %get-tuple-element.34.refs_2_, f32[1,512]{1,0:T(1,128)} %bitcast.14, bf16[1040,128]{1,0:T(8,128)(2,1)} %bundle.1.refs_0_.refs_4_, bf16[1040,128]{1,0:T(8,128)(2,1)} %copy-done.2, ...), custom_call_target="tpu_custom_call" | custom-call | tf_op jit(solution)/shard_map/node/pallas_call | solution.py:49
  (9 shorter events, 0.0 us)
Async XLA Ops:
  1.7 17.4 %all-to-all-start = ((s32[8,8,128]{2,1,0:T(8,128)}), s32[8,8,128]{2,1,0:T(8,128)S(1)}, u32[]{:S(2)}, u32[]{:S(2)}) async-start(s32[8,8,128]{2,1,0:T(8,128)} %get-tuple-element.21), calls=%async_computation | async-start | bytes 65536 | tf_op jit(solution)/shard_map/all_to_all | solution.py:245
  19.1 14.2 %copy-start.4 = (s32[8,8,128]{2,1,0:T(8,128)}, s32[8,8,128]{2,1,0:T(8,128)S(1)}, u32[]{:S(2)}) copy-start(s32[8,8,128]{2,1,0:T(8,128)S(1)} %all-to-all-done.refs_0_) | copy-start | bytes 98308
  21.2 21.1 %all-to-all-start.1 = ((bf16[8,32,128]{2,1,0:T(8,128)(2,1)}), bf16[8,32,128]{2,1,0:T(8,128)(2,1)S(1)}, u32[]{:S(2)}, u32[]{:S(2)}) async-start(bf16[8,32,128]{2,1,0:T(8,128)(2,1)} %offer.1), calls=%async_computation.1 | async-start | bytes 131072 | tf_op jit(solution)/shard_map/all_to_all | solution.py:254
  33.3 14.5 %collective-permute-start.2 = (bf16[1040,128]{1,0:T(8,128)(2,1)}, bf16[1040,128]{1,0:T(8,128)(2,1)S(1)}, u32[]{:S(2)}, u32[]{:S(2)}) collective-permute-start(bf16[1040,128]{1,0:T(8,128)(2,1)} %bundle.1.refs_0_.refs_4_), channel_id=1, source_target_pairs={{0,3},{1,0},{2,1},{3,2},{4,7},{5,4},{6,5},{7,6},{8,11},{9,8},{10,9... | collective-permute-start | bytes 798728 | tf_op jit(solution)/shard_map/ppermute | solution.py:263
  35.2 12.6 %collective-permute-start.1 = (bf16[1040,128]{1,0:T(8,128)(2,1)}, bf16[1040,128]{1,0:T(8,128)(2,1)S(1)}, u32[]{:S(2)}, u32[]{:S(2)}) collective-permute-start(bf16[1040,128]{1,0:T(8,128)(2,1)} %bundle.1.refs_0_.refs_4_), channel_id=1, source_target_pairs={{0,2},{1,3},{2,0},{3,1},{4,6},{5,7},{6,4},{7,5},{8,10},{9,11},{10,... | collective-permute-start | bytes 798728 | tf_op jit(solution)/shard_map/ppermute | solution.py:263
  39.1 11.2 %collective-permute-start = (bf16[1040,128]{1,0:T(8,128)(2,1)}, bf16[1040,128]{1,0:T(8,128)(2,1)S(1)}, u32[]{:S(2)}, u32[]{:S(2)}) collective-permute-start(bf16[1040,128]{1,0:T(8,128)(2,1)} %bundle.1.refs_0_.refs_4_), channel_id=1, source_target_pairs={{0,1},{1,2},{2,3},{3,0},{4,5},{5,6},{6,7},{7,4},{8,9},{9,10},{10,1... | collective-permute-start | bytes 798728 | tf_op jit(solution)/shard_map/ppermute | solution.py:263
  47.8 9.3 %copy-start = (bf16[1040,128]{1,0:T(8,128)(2,1)}, bf16[1040,128]{1,0:T(8,128)(2,1)S(1)}, u32[]{:S(2)}) copy-start(bf16[1040,128]{1,0:T(8,128)(2,1)S(1)} %collective-permute-done.2.refs_3_.refs_7_) | copy-start | bytes 798724
  47.8 9.3 %copy-start.1 = (bf16[1040,128]{1,0:T(8,128)(2,1)}, bf16[1040,128]{1,0:T(8,128)(2,1)S(1)}, u32[]{:S(2)}) copy-start(bf16[1040,128]{1,0:T(8,128)(2,1)S(1)} %collective-permute-done.1.refs_2_.refs_6_) | copy-start | bytes 798724
  50.3 6.8 %copy-start.2 = (bf16[1040,128]{1,0:T(8,128)(2,1)}, bf16[1040,128]{1,0:T(8,128)(2,1)S(1)}, u32[]{:S(2)}) copy-start(bf16[1040,128]{1,0:T(8,128)(2,1)S(1)} %collective-permute-done.refs_1_.refs_5_) | copy-start | bytes 798724
  50.3 17.3 %all-to-all-start.2 = ((bf16[8,128,128]{2,1,0:T(8,128)(2,1)}), bf16[8,128,128]{2,1,0:T(8,128)(2,1)S(1)}, u32[]{:S(2)}, u32[]{:S(2)}) async-start(bf16[8,128,128]{2,1,0:T(8,128)(2,1)} %select.1), calls=%async_computation.2 | async-start | bytes 524288 | tf_op jit(solution)/shard_map/all_to_all | solution.py:275
  67.6 0.7 copy-start.3

commit v3 on v2

v3 whole, which is shorter than its diff:
```python
import jax
import jax.numpy as jnp
from jax import lax
from jax.experimental import pallas as pl
from jax.experimental.pallas import tpu as pltpu
from jax.sharding import Mesh
from jax.sharding import PartitionSpec as P

NODE = ("y", "z", "core")
EPS = 1e-05
TAIL = 16

LIMIT = 60 << 20
ROOM = 40 << 20
WEIGHT = 10**10
bf16, f32, i32 = jnp.bfloat16, jnp.float32, jnp.int32


def call(body, operands, outs, scratch=(), scalars=(), part={}, flops=0, moved=0, limit=LIMIT):
    count = len(operands)
    space = [pltpu.SMEM if i in scalars else pltpu.VMEM for i in range(count)]

    def kernel(*refs):
        sources, rest = refs[:count], refs[count:]
        results, held, rest = rest[: len(outs)], rest[len(outs) :][:count], rest[len(outs) + count :]
        sems, extra = rest[-1], rest[:-1]
        copies = [
            pltpu.make_async_copy(
                source.at[part[i][0]] if i in part else source, target, sems.at[i]
            )
            for i, (source, target) in enumerate(zip(sources, held))
        ]
        for copy in copies:
            copy.start()

        def ready(i):
            def get():
                if copies[i] is not None:
                    copies[i].wait()
                    copies[i] = None
                return held[i]

            return get

        gets = [ready(i) for i in range(count)]
        body(*gets, *results, *extra)
        for get in gets:
            get()

    return pl.pallas_call(
        kernel,
        out_shape=[jax.ShapeDtypeStruct(shape, kind) for shape, kind in outs],
        in_specs=[pl.BlockSpec(memory_space=pltpu.HBM)] * count,
        out_specs=[pl.BlockSpec(memory_space=pltpu.VMEM)] * len(outs),
        scratch_shapes=[
            kind(part[i][1] if i in part else v.shape, v.dtype)
            for i, (kind, v) in enumerate(zip(space, operands))
        ]
        + list(scratch)
        + [pltpu.SemaphoreType.DMA((count,))],
        compiler_params=pltpu.CompilerParams(vmem_limit_bytes=limit),
        cost_estimate=pl.CostEstimate(flops=flops, bytes_accessed=moved, transcendentals=0),
        name=body.__name__,
    )(*operands)


def matmul(left, right):
    return jnp.dot(left, right, preferred_element_type=f32)


def silu(value):
    half = 0.5 * value
    return half + half * jnp.tanh(half)


def gather(block, beside=None):
    near, far = [[0, 1], [2, 3]], [[0, 3], [1, 2]]
    turned = [[0, 1], [3, 2]]
    for first, second in ((near, far), (far, turned)):
        groups = first + [[4 + i for i in group] for group in second]
        if block.ndim > 2 and beside is not None:
            block, beside = lax.optimization_barrier((block, beside))
        block = lax.all_gather(
            block, ("core", "sect"), axis=0, axis_index_groups=groups, tiled=block.ndim > 2
        )
    return block if beside is None else (block, beside)


def ordered(whole):
    core = lax.axis_index("core")
    return [whole.at[0], whole.at[1 + core], whole.at[2 + core], whole.at[3 - 2 * core]]


def offer(export, latent, w1, b1, w2, b2, out):
    rows = latent().shape[1]
    offers = out.shape[1]
    table = jnp.broadcast_to(export()[...].astype(f32), (offers, offers))
    on = lax.broadcasted_iota(i32, table.shape, 0) == lax.broadcasted_iota(i32, table.shape, 1)
    column = jnp.sum(jnp.where(on, table, 0.0), 1, keepdims=True).astype(i32)
    chosen = column == lax.broadcasted_iota(i32, (offers, rows), 1)
    chosen = jnp.where(chosen, 1.0, 0.0).astype(bf16)
    every = jnp.concatenate([part[...] for part in ordered(latent())], 1)
    picked = matmul(chosen, every).astype(bf16)
    hidden = silu(matmul(picked, w1()[...]) + b1()[...]).astype(bf16)
    message = (matmul(hidden, w2()[...]) + b2()[...]).astype(bf16)
    for peer in range(out.shape[0]):
        out[peer] = message


def select(wanted, offered, out):
    wanted, offered = wanted(), offered()
    n_z, takes, lanes = wanted.shape
    column = 2 * n_z
    n_y = lanes // column
    offers = offered.shape[0] // (2 * n_y)
    quad = 128 // offers
    half = offered.shape[0] // 2
    shift = lax.rem(lanes - 2 * lax.axis_index("z"), lanes)
    lane = lax.broadcasted_iota(i32, (takes, 128), 1)
    blank = jnp.zeros((takes, 128), f32)
    for q in range(n_y // quad):
        sources = jnp.concatenate(
            [offered[pl.ds(c * half + q * 128, 128), :] for c in range(2)], 0
        )
        chosen = []
        for peer in range(n_z):
            table = pltpu.roll(wanted[peer], shift, 1)
            for part in range(quad):
                at = (q * quad + part) * column
                first, second = [
                    jnp.where(
                        table[:, at + c : at + c + 1] + part * offers == lane, 1.0, 0.0
                    )
                    for c in range(2)
                ]
                chosen.append(jnp.concatenate([first, blank], 1))
                chosen.append(jnp.concatenate([blank, second], 1))
        chosen = jnp.concatenate(chosen, 0).astype(bf16)
        rows = matmul(chosen, sources).astype(bf16)
        depth = quad * 2 * takes
        for peer in range(n_z):
            out[peer, pl.ds(q * depth, depth), :] = rows[peer * depth : (peer + 1) * depth]


def send(latent, w1, b1, w2, b2, node_w2, node_b2, message, side):
    rows = latent().shape[1]
    blocks = ordered(latent())
    step = rows // 2
    for r in range(0, rows, step):
        at = pl.ds(r, step)
        x = jnp.concatenate([block[at, :] for block in blocks], 1)
        hidden = silu(matmul(x, w1()[...]) + b1()[...]).astype(bf16)
        message[at, :] = (matmul(hidden, w2()[...]) + b2()[...]).astype(bf16)
    width = node_w2().shape[0]
    side[pl.ds(0, width), :] = node_w2()[...]
    row = node_b2()[...].astype(f32)
    side[pl.ds(width, TAIL), :] = jnp.broadcast_to(row, (TAIL, row.shape[1])).astype(bf16)


def above(latent, weight, side0, side1, upper, pair):
    rows = latent().shape[1]
    blocks = ordered(latent())
    step = rows // 2
    for r in range(0, rows, step):
        at = pl.ds(r, step)
        x = jnp.concatenate([block[at, :] for block in blocks], 1)
        upper[at, :] = matmul(x, weight()[...])
    pair[0] = side0()[...]
    pair[1] = side1()[...]


def tiles(source, message, halo, *rest):
    *weight, out, extended = rest
    tile, share = extended.shape[1:]
    own = message().shape[0] // tile
    for b in range(own):
        extended[b] = message()[pl.ds(b * tile, tile), :]
    peers, rows, _ = halo().shape
    run = tile // peers
    for b in range(rows // run):
        for peer in range(peers):
            extended[own + b, pl.ds(peer * run, run), :] = halo()[peer, pl.ds(b * run, run), :]
    src = source()
    group = 4
    for b, block in enumerate(weight):
        terms = block().shape[0]
        total = jnp.zeros((tile, share), f32)
        for k in range(0, terms, group):
            left = jnp.concatenate([block()[k + g] for g in range(group)], 1)
            right = jnp.concatenate([extended[src[b, k + g]] for g in range(group)], 0)
            total = total + matmul(left, right)
        out[pl.ds(b * tile, tile), :] = total.astype(bf16)


def node(lower_w, b1, *rest):
    *chunks, pair0, pair1, latent, gain, bias, out = rest
    sides = []
    r = 0
    for aggregate, upper in zip(chunks[::2], chunks[1::2]):
        parts, step, share = aggregate().shape
        width = share * parts
        at = pl.ds(r, step)
        r += step
        x = jnp.concatenate([part[...] for part in ordered(aggregate())], 1)
        hidden = silu(upper()[...] + matmul(x, lower_w()[...]) + b1()[...]).astype(bf16)
        if not sides:
            sides = [pair()[p] for pair in (pair0, pair1) for p in range(2)]
            w2 = jnp.concatenate([side[:width] for side in sides], 1)
            b2 = jnp.concatenate([side[width : width + 1] for side in sides], 1).astype(f32)
        every = matmul(hidden, w2) + b2
        split = [every[:, p * share : (p + 1) * share] for p in range(parts)]
        mine = split[0]
        total = jnp.sum(sum(split), 1, keepdims=True)
        squares = jnp.sum(sum(v * v for v in split), 1, keepdims=True)
        mean = total * (1.0 / width)
        var = squares * (1.0 / width) - mean * mean
        normed = (mine - mean) * lax.rsqrt(var + EPS)
        result = latent()[at, :].astype(f32) + gain()[...] * normed + bias()[...]
        out[at, :] = result.astype(bf16)


def local(
    latent,
    export_rows,
    halo_slots,
    tile_src,
    tile_weight,
    send_w1,
    send_b1,
    send_w2,
    send_b2,
    node_w1,
    node_b1,
    node_w2,
    node_b2,
    ln_gain,
    ln_bias,
):
    rows, share = latent.shape
    width = send_w1.shape[0]
    offers = export_rows.shape[1]
    takes = halo_slots.shape[2]
    n_y, n_z, n_core, n_sect = (lax.axis_size(name) for name in NODE + ("sect",))
    tile = tile_weight.shape[-1]
    send_b1, send_b2, node_b1, node_b2, ln_gain, ln_bias = (
        v[None] for v in (send_b1, send_b2, node_b1, node_b2, ln_gain, ln_bias)
    )

    sender = (send_w1, send_b1, send_w2, send_b2)

    slots = jnp.swapaxes(halo_slots[0], 0, 1)
    wanted = lax.all_to_all(jnp.broadcast_to(slots[None], (n_z,) + slots.shape), "z", 0, 0)
    whole = gather(latent)
    whole, wanted = lax.optimization_barrier((whole, wanted))
    (offered,) = call(
        offer, (export_rows, whole, *sender), [((n_y, offers, share), bf16)]
    )

    offered, later = lax.optimization_barrier((offered, whole))
    offered = lax.all_to_all(offered, "y", 0, 0).reshape(n_y * offers, share)
    message, side = call(
        send,
        (later, *sender, node_w2, node_b2),
        [((rows, share), bf16), ((width + TAIL, share), bf16)],
        flops=WEIGHT,
    )
    other = lax.ppermute(side, "sect", [(i, i ^ 1) for i in range(n_sect)])
    offered = lax.all_gather(offered, "core", axis=0, tiled=True)
    (halo,) = call(
        select,
        (wanted, offered),
        [((n_z, n_y * n_core * takes, share), bf16)],
        flops=2 * WEIGHT,
        limit=ROOM,
    )

    halo, other, later = lax.optimization_barrier((halo, other, later))
    halo = lax.all_to_all(halo, "z", 0, 0)
    upper, pair = call(
        above,
        (later, node_w1, side, other),
        [((rows, width), f32), ((2, width + TAIL, share), bf16)],
        part={1: (pl.ds(0, width), (width, width))},
        flops=WEIGHT,
    )
    others = lax.ppermute(pair, "sect", [(i, n_sect - 1 - i) for i in range(n_sect)])

    blocks, terms = tile_src.shape
    (aggregate,) = call(
        tiles,
        (tile_src, message, halo) + (tile_weight,) * blocks,
        [((rows, share), bf16)],
        [pltpu.VMEM((rows // tile + n_y, tile, share), bf16)],
        scalars=(0,),
        part={3 + b: (b, (terms, tile, tile)) for b in range(blocks)},
        limit=ROOM,
        flops=2 * WEIGHT,
    )
    aggregate, others = gather(aggregate, others)

    step = rows // 2
    part = {0: (pl.ds(width, width), (width, width))}
    for c in range(2):
        at = pl.ds(c * step, step)
        part[2 + 2 * c] = ((slice(None), at), (n_sect, step, share))
        part[3 + 2 * c] = (at, (step, width))
    (updated,) = call(
        node,
        (node_w1, node_b1)
        + (aggregate, upper) * 2
        + (pair, others, latent, ln_gain, ln_bias),
        [((rows, share), bf16)],
        part=part,
        limit=ROOM,
    )
    return updated


def solution(mesh):
    n_mesh, n_sect = mesh.devices.shape
    n_y = n_z = int(round((n_mesh // 2) ** 0.5))
    grid = Mesh(mesh.devices.reshape(n_y, n_z, 2, n_sect), NODE + ("sect",))
    in_specs = (
        P(NODE, "sect"),
        P(NODE, None),
        P(NODE, None, None),
        P(NODE, None),
        P(NODE, None, None, None),
        P(),
        P(),
        P(None, "sect"),
        P("sect"),
        P(),
        P(),
        P(None, "sect"),
        P("sect"),
        P("sect"),
        P("sect"),
    )
    out_specs = P(NODE, "sect")
    return jax.shard_map(local, mesh=grid, in_specs=in_specs, out_specs=out_specs, check_vma=False)
```

time: 90.2 us -> 85.6 us (0.949); the launches traced: 88.5 us -> 85.1 us
  blocking collectives: 25.2 us -> 30 us
  Pallas kernels: 18.9 us -> 14.2 us
  starting transfers between devices: 33.2 us -> 29 us
    all_gather x2 -> x4, blocking collectives: 10.3 us -> 28.1 us  [gather(): lax.all_gather(block, ('core', 'sect'), axis=0, axis_index_groups=groups,...]
    all_to_all x1 -> x0, blocking collectives: 12.8 us -> none  [local(): aggregate = lax.all_to_all(aggregate, 'sect', 0, 0)]
    pallas_call x7 -> x6, Pallas kernels: 18.9 us -> 14.2 us  [call(): pl.pallas_call(kernel, out_shape=[jax.ShapeDtypeStruct(shape, kind) for s...]
    ppermute x3 -> x2, starting transfers between devices: 8.97 us -> 4.31 us  [the longest x1 2.39 us: local(): lax.ppermute(pair, 'sect', [(i, n_sect - 1 - i) for i in range(n_sect)])]
    ppermute x3 -> x2, waiting for transfers between devices: 3.81 us -> 0.01 us  [the longest x1 0.01 us: local(): other = lax.ppermute(side, 'sect', [(i, i ^ 1) for i in range(n_sect)])]
    all_to_all x3, waiting for transfers between devices: 6.62 us -> 10.4 us  [the longest x1 6.85 us: local(): halo = lax.all_to_all(halo, 'z', 0, 0)]
    broadcast_in_dim x0 -> x1, local copies, waits for them, and re-layouts: none -> 1.3 us  [local(): jnp.broadcast_to(slots[None], (n_z,) + slots.shape)]
  transfers between devices with their start and end apart: 6 -> 5, of which waited for: 3 -> 2; matrix products, arithmetic and copies ran while one was open for 0% -> 0% of each run, Pallas kernels for 4% -> 7%
where the time goes in v3:
time: 85.6 us; the launch traced here: 85.1 us
  blocking collectives  30 us (35%)
  starting transfers between devices  29 us (34%)
  Pallas kernels  14.2 us (17%)
  waiting for transfers between devices  10.4 us (12%)
  local copies, waits for them, and re-layouts  1.37 us (2%)
    all_gather x4, blocking collectives, gather(): lax.all_gather(block, ('core', 'sect'), axis=0, axis_index_groups=groups,...  28.1 us
    pallas_call x6, Pallas kernels, call(): pl.pallas_call(kernel, out_shape=[jax.ShapeDtypeStruct(shape, kind) for s...  14.2 us
    all_to_all x1, starting transfers between devices, local(): lax.all_to_all(jnp.broadcast_to(slots[None], (n_z,) + slots.shape), 'z',...  10.3 us
    all_to_all x1, starting transfers between devices, local(): halo = lax.all_to_all(halo, 'z', 0, 0)  7.22 us
    all_to_all x1, starting transfers between devices, local(): offered = lax.all_to_all(offered, 'y', 0, 0).reshape(n_y * offers, share)  7.11 us
    all_to_all x1, waiting for transfers between devices, local(): halo = lax.all_to_all(halo, 'z', 0, 0)  6.85 us
    all_to_all x1, waiting for transfers between devices, local(): offered = lax.all_to_all(offered, 'y', 0, 0).reshape(n_y * offers, share)  3.54 us
    ppermute x1, starting transfers between devices, local(): lax.ppermute(pair, 'sect', [(i, n_sect - 1 - i) for i in range(n_sect)])  2.39 us
  transfers between devices with their start and end apart: 5, of which 2 were waited for; matrix products, arithmetic and copies ran while one was open for 0% of the time, Pallas kernels for 7%

profile of v3, /device:TPU:6, one launch (start us, length us, event | category | flops | bytes accessed | tf_op | source)
XLA Modules:
  0.0 85.1 jit_solution(8012766932626450004)
XLA Ops:
  0.0 1.3 %broadcast_in_dim.25 = s32[8,8,128]{2,1,0:T(8,128)} broadcast(s32[8,128]{1,0:T(8,128)} %bitcast.18), dimensions={1,2} | broadcast | bytes 36864 | tf_op jit(solution)/shard_map/broadcast_in_dim | solution.py:252
  1.3 10.3 %all-to-all-start = ((s32[8,8,128]{2,1,0:T(8,128)}), s32[8,8,128]{2,1,0:T(8,128)S(1)}, u32[]{:S(2)}, u32[]{:S(2)}) async-start(s32[8,8,128]{2,1,0:T(8,128)} %broadcast_in_dim.25), calls=%async_computation | async-start | bytes 65536 | tf_op jit(solution)/shard_map/all_to_all | solution.py:252
  11.6 5.8 %all-gather = bf16[1024,128]{1,0:T(8,128)(2,1)S(1)} all-gather(bf16[512,128]{1,0:T(8,128)(2,1)} %refs_8_.1), channel_id=2, replica_groups={{0,1},{2,3},{4,7},{5,6},{8,9},{10,11},{12,15},{13,14},{16,17},{18,19},{..., dimensions={0}, use_global_device_ids=true | all-gather | bytes 393216 | tf_op jit(solution)/shard_map/all_gather | solution.py:83
  17.5 8.4 %all_gather.23.refs_1_.refs_0_ = bf16[4,512,128]{2,1,0:T(8,128)(2,1)} all-gather(bf16[2,512,128]{2,1,0:T(8,128)(2,1)S(1)} %bitcast.16), channel_id=1, replica_groups={{0,3},{1,2},{4,5},{7,6},{8,11},{9,10},{12,13},{15,14},{16,19},{17,18},{..., dimensions={0}, use_global_device_ids=true | all-gather | bytes 786432 | tf_op jit(solution)/shard_map/all_gather | solution.py:83
  25.8 2.4 %offer.1 = bf16[8,32,128]{2,1,0:T(8,128)(2,1)} custom-call(s32[1,32]{1,0:T(1,128)} %refs_0_.3, bf16[4,512,128]{2,1,0:T(8,128)(2,1)} %all_gather.23.refs_1_.refs_0_, bf16[512,512]{1,0:T(8,128)(2,1)} %refs_1_.2, f32[1,512]{1,0:T(1,128)} %bitcast.19, bf16[512,128]{1,0:T(8,128)(2,1)} %refs_3_.2, f32[1,128]{1,0:T(1,128)} %bitcast.21), custom_call_target="tpu_custom_call" | custom-call | tf_op jit(solution)/shard_map/offer/pallas_call | solution.py:50
  28.2 7.1 %all-to-all-start.1 = ((bf16[8,32,128]{2,1,0:T(8,128)(2,1)}), bf16[8,32,128]{2,1,0:T(8,128)(2,1)S(1)}, u32[]{:S(2)}, u32[]{:S(2)}) async-start(bf16[8,32,128]{2,1,0:T(8,128)(2,1)} %offer.1), calls=%async_computation.1 | async-start | bytes 131072 | tf_op jit(solution)/shard_map/all_to_all | solution.py:260
  35.3 2.9 %send.1 = (bf16[512,128]{1,0:T(8,128)(2,1)}, bf16[528,128]{1,0:T(8,128)(2,1)}) custom-call(bf16[4,512,128]{2,1,0:T(8,128)(2,1)} %all_gather.23.refs_1_.refs_0_, bf16[512,512]{1,0:T(8,128)(2,1)} %refs_1_.2, f32[1,512]{1,0:T(1,128)} %bitcast.20, bf16[512,128]{1,0:T(8,128)(2,1)} %refs_3_.2, f32[1,128]{1,0:T(1,128)} %bitcast.22, bf16[512,128]{1,0:T(8,128)(2,1)} %refs_5_.2, ...), custom_call_target="tpu_custom_call" | custom-call | flops 10000000000 | tf_op jit(solution)/shard_map/send/pallas_call | solution.py:50
  38.2 1.9 %collective-permute-start = (bf16[528,128]{1,0:T(8,128)(2,1)}, bf16[528,128]{1,0:T(8,128)(2,1)S(1)}, u32[]{:S(2)}, u32[]{:S(2)}) collective-permute-start(bf16[528,128]{1,0:T(8,128)(2,1)} %get-tuple-element.23.refs_2_), channel_id=1, source_target_pairs={{0,1},{1,0},{2,3},{3,2},{4,5},{5,4},{6,7},{7,6},{8,9},{9,8},{10,11... | collective-permute-start | bytes 405512 | tf_op jit(solution)/shard_map/ppermute | solution.py:267
  40.2 3.5 %all-to-all-done.1 = bf16[8,32,128]{2,1,0:T(8,128)(2,1)S(1)} async-done(((bf16[8,32,128]{2,1,0:T(8,128)(2,1)}), bf16[8,32,128]{2,1,0:T(8,128)(2,1)S(1)}, u32[]{:S(2)}, u32[]{:S(2)}) %all-to-all-start.1) | async-done | bytes 65568 | tf_op jit(solution)/shard_map/all_to_all | solution.py:260
  43.7 1.9 %all_gather.24.refs_1_ = bf16[512,128]{1,0:T(8,128)(2,1)S(1)} all-gather(bf16[256,128]{1,0:T(8,128)(2,1)S(1)} %bitcast.17), channel_id=1, replica_groups=mesh['y'=8,'z'=8,'core'=2,'sect'=4] {'core'}, dimensions={0}, use_global_device_ids=true | all-gather | bytes 196608 | tf_op jit(solution)/shard_map/all_gather | solution.py:268
  45.6 1.4 %select.1 = bf16[8,128,128]{2,1,0:T(8,128)(2,1)} custom-call(s32[8,8,128]{2,1,0:T(8,128)S(1)} %all-to-all-done.refs_0_, bf16[512,128]{1,0:T(8,128)(2,1)S(1)} %all_gather.24.refs_1_), custom_call_target="tpu_custom_call" | custom-call | flops 20000000000 | tf_op jit(solution)/shard_map/select/pallas_call | solution.py:50
  47.0 7.2 %all-to-all-start.2 = ((bf16[8,128,128]{2,1,0:T(8,128)(2,1)}), bf16[8,128,128]{2,1,0:T(8,128)(2,1)S(1)}, u32[]{:S(2)}, u32[]{:S(2)}) async-start(bf16[8,128,128]{2,1,0:T(8,128)(2,1)} %select.1), calls=%async_computation.2 | async-start | bytes 524288 | tf_op jit(solution)/shard_map/all_to_all | solution.py:278
  54.3 0.0 copy-start.7
  54.3 0.0 copy-start.8
  54.3 0.0 copy-start.9
  54.3 2.9 %above.1 = (f32[512,512]{1,0:T(8,128)}, bf16[2,528,128]{2,1,0:T(8,128)(2,1)}) custom-call(bf16[4,512,128]{2,1,0:T(8,128)(2,1)} %all_gather.23.refs_1_.refs_0_, bf16[1024,512]{1,0:T(8,128)(2,1)} %refs_0_.5, bf16[528,128]{1,0:T(8,128)(2,1)} %get-tuple-element.23.refs_2_, bf16[528,128]{1,0:T(8,128)(2,1)} %copy-done.10), custom_call_target="tpu_custom_call" | custom-call | flops 10000000000 | tf_op jit(solution)/shard_map/above/pallas_call | solution.py:50
  57.2 2.4 %collective-permute-start.1 = (bf16[2,528,128]{2,1,0:T(8,128)(2,1)}, bf16[2,528,128]{2,1,0:T(8,128)(2,1)S(1)}, u32[]{:S(2)}, u32[]{:S(2)}) collective-permute-start(bf16[2,528,128]{2,1,0:T(8,128)(2,1)} %get-tuple-element.27.refs_6_), channel_id=1, source_target_pairs={{0,3},{1,2},{2,1},{3,0},{4,7},{5,6},{6,5},{7,4},{8,11},{9,10},{10,... | collective-permute-start | bytes 811016 | tf_op jit(solution)/shard_map/ppermute | solution.py:286
  59.6 6.9 %all-to-all-done.2.refs_2_ = bf16[8,128,128]{2,1,0:T(8,128)(2,1)S(1)} async-done(((bf16[8,128,128]{2,1,0:T(8,128)(2,1)}), bf16[8,128,128]{2,1,0:T(8,128)(2,1)S(1)}, u32[]{:S(2)}, u32[]{:S(2)}) %all-to-all-start.2) | async-done | bytes 262176 | tf_op jit(solution)/shard_map/all_to_all | solution.py:278
  66.5 0.0 copy-start.4
  66.5 0.0 copy-start.5
  66.5 1.8 %tiles.1 = bf16[512,128]{1,0:T(8,128)(2,1)S(1)} custom-call(s32[4,16]{1,0:T(4,128)S(1)} %copy-done.8, bf16[512,128]{1,0:T(8,128)(2,1)S(1)} %copy-done.9, bf16[8,128,128]{2,1,0:T(8,128)(2,1)S(1)} %all-to-all-done.2.refs_2_, bf16[4,16,128,128]{3,2,1,0:T(8,128)(2,1)S(1)} %copy-done.7, bf16[4,16,128,128]{3,2,1,0:T(8,128)(2,1)S(1)} %copy-done.7, ...), custom_call_target="tpu_custom_call" | custom-call | flops 20000000000 | tf_op jit(solution)/shard_map/tiles/pallas_call | solution.py:50
  68.4 5.6 %all-gather.1 = bf16[1024,128]{1,0:T(8,128)(2,1)S(1)} all-gather(bf16[512,128]{1,0:T(8,128)(2,1)S(1)} %tiles.1), channel_id=3, replica_groups={{0,1},{2,3},{4,7},{5,6},{8,9},{10,11},{12,15},{13,14},{16,17},{18,19},{..., dimensions={0}, use_global_device_ids=true | all-gather | bytes 393216 | tf_op jit(solution)/shard_map/all_gather | solution.py:83
  74.0 8.2 %all_gather.27.refs_2_.refs_4_ = bf16[4,512,128]{2,1,0:T(8,128)(2,1)S(1)} all-gather(bf16[2,512,128]{2,1,0:T(8,128)(2,1)S(1)} %bitcast.15), channel_id=1, replica_groups={{0,3},{1,2},{4,5},{7,6},{8,11},{9,10},{12,13},{15,14},{16,19},{17,18},{..., dimensions={0}, use_global_device_ids=true | all-gather | bytes 786432 | tf_op jit(solution)/shard_map/all_gather | solution.py:83
  82.3 2.8 %node.1 = bf16[512,128]{1,0:T(8,128)(2,1)} custom-call(bf16[1024,512]{1,0:T(8,128)(2,1)S(1)} %copy-done.1, f32[1,512]{1,0:T(1,128)S(1)} %bitcast.12, bf16[4,512,128]{2,1,0:T(8,128)(2,1)S(1)} %all_gather.27.refs_2_.refs_4_, f32[512,512]{1,0:T(8,128)S(1)} %copy-done, bf16[4,512,128]{2,1,0:T(8,128)(2,1)S(1)} %all_gather.27.refs_2_.refs_4_, ...), custom_call_target="tpu_custom_call" | custom-call | tf_op jit(solution)/shard_map/node/pallas_call | solution.py:50
  (20 shorter events, 0.0 us)
Async XLA Ops:
  1.3 24.5 %all-to-all-start = ((s32[8,8,128]{2,1,0:T(8,128)}), s32[8,8,128]{2,1,0:T(8,128)S(1)}, u32[]{:S(2)}, u32[]{:S(2)}) async-start(s32[8,8,128]{2,1,0:T(8,128)} %broadcast_in_dim.25), calls=%async_computation | async-start | bytes 65536 | tf_op jit(solution)/shard_map/all_to_all | solution.py:252
  28.2 15.5 %all-to-all-start.1 = ((bf16[8,32,128]{2,1,0:T(8,128)(2,1)}), bf16[8,32,128]{2,1,0:T(8,128)(2,1)S(1)}, u32[]{:S(2)}, u32[]{:S(2)}) async-start(bf16[8,32,128]{2,1,0:T(8,128)(2,1)} %offer.1), calls=%async_computation.1 | async-start | bytes 131072 | tf_op jit(solution)/shard_map/all_to_all | solution.py:260
  38.2 8.8 %collective-permute-start = (bf16[528,128]{1,0:T(8,128)(2,1)}, bf16[528,128]{1,0:T(8,128)(2,1)S(1)}, u32[]{:S(2)}, u32[]{:S(2)}) collective-permute-start(bf16[528,128]{1,0:T(8,128)(2,1)} %get-tuple-element.23.refs_2_), channel_id=1, source_target_pairs={{0,1},{1,0},{2,3},{3,2},{4,5},{5,4},{6,7},{7,6},{8,9},{9,8},{10,11... | collective-permute-start | bytes 405512 | tf_op jit(solution)/shard_map/ppermute | solution.py:267
  47.0 7.2 %copy-start.10 = (bf16[528,128]{1,0:T(8,128)(2,1)}, bf16[528,128]{1,0:T(8,128)(2,1)S(1)}, u32[]{:S(2)}) copy-start(bf16[528,128]{1,0:T(8,128)(2,1)S(1)} %collective-permute-done.refs_3_) | copy-start | bytes 405508
  47.0 19.4 %all-to-all-start.2 = ((bf16[8,128,128]{2,1,0:T(8,128)(2,1)}), bf16[8,128,128]{2,1,0:T(8,128)(2,1)S(1)}, u32[]{:S(2)}, u32[]{:S(2)}) async-start(bf16[8,128,128]{2,1,0:T(8,128)(2,1)} %select.1), calls=%async_computation.2 | async-start | bytes 524288 | tf_op jit(solution)/shard_map/all_to_all | solution.py:278
  54.3 12.2 %copy-start.7 = (bf16[4,16,128,128]{3,2,1,0:T(8,128)(2,1)S(1)}, bf16[4,16,128,128]{3,2,1,0:T(8,128)(2,1)}, u32[]{:S(2)}) copy-start(bf16[4,16,128,128]{3,2,1,0:T(8,128)(2,1)} %refs_6_.1) | copy-start | bytes 6291460
  54.3 12.2 %copy-start.8 = (s32[4,16]{1,0:T(4,128)S(1)}, s32[4,16]{1,0:T(4,128)}, u32[]{:S(2)}) copy-start(s32[4,16]{1,0:T(4,128)} %refs_0_.4) | copy-start | bytes 772
  54.3 12.2 %copy-start.9 = (bf16[512,128]{1,0:T(8,128)(2,1)S(1)}, bf16[512,128]{1,0:T(8,128)(2,1)}, u32[]{:S(2)}) copy-start(bf16[512,128]{1,0:T(8,128)(2,1)} %get-tuple-element.20.refs_1_) | copy-start | bytes 393220
  57.2 16.8 %collective-permute-start.1 = (bf16[2,528,128]{2,1,0:T(8,128)(2,1)}, bf16[2,528,128]{2,1,0:T(8,128)(2,1)S(1)}, u32[]{:S(2)}, u32[]{:S(2)}) collective-permute-start(bf16[2,528,128]{2,1,0:T(8,128)(2,1)} %get-tuple-element.27.refs_6_), channel_id=1, source_target_pairs={{0,3},{1,2},{2,1},{3,0},{4,7},{5,6},{6,5},{7,4},{8,11},{9,10},{10,... | collective-permute-start | bytes 811016 | tf_op jit(solution)/shard_map/ppermute | solution.py:286
  66.5 15.8 %copy-start = (f32[512,512]{1,0:T(8,128)S(1)}, f32[512,512]{1,0:T(8,128)}, u32[]{:S(2)}) copy-start(f32[512,512]{1,0:T(8,128)} %get-tuple-element.29.refs_3_.refs_5_) | copy-start | bytes 3145732
  66.5 15.8 %copy-start.1 = (bf16[1024,512]{1,0:T(8,128)(2,1)S(1)}, bf16[1024,512]{1,0:T(8,128)(2,1)}, u32[]{:S(2)}) copy-start(bf16[1024,512]{1,0:T(8,128)(2,1)} %refs_0_.5) | copy-start | bytes 3145732
  66.5 15.8 %copy-start.2 = (bf16[512,128]{1,0:T(8,128)(2,1)S(1)}, bf16[512,128]{1,0:T(8,128)(2,1)}, u32[]{:S(2)}) copy-start(bf16[512,128]{1,0:T(8,128)(2,1)} %refs_8_.1) | copy-start | bytes 393220
  66.5 15.8 %copy-start.3 = (bf16[2,528,128]{2,1,0:T(8,128)(2,1)S(1)}, bf16[2,528,128]{2,1,0:T(8,128)(2,1)}, u32[]{:S(2)}) copy-start(bf16[2,528,128]{2,1,0:T(8,128)(2,1)} %get-tuple-element.27.refs_6_) | copy-start | bytes 811012
  66.5 15.8 %copy-start.4 = (f32[512]{0:T(512)S(1)}, f32[512]{0:T(512)}, u32[]{:S(2)}) copy-start(f32[512]{0:T(512)} %param.25) | copy-start | bytes 6148
  66.5 15.8 %copy-start.5 = (f32[128]{0:T(128)S(1)}, f32[128]{0:T(128)}, u32[]{:S(2)}) copy-start(f32[128]{0:T(128)} %param.28) | copy-start | bytes 1540
  66.5 15.8 %copy-start.6 = (f32[128]{0:T(128)S(1)}, f32[128]{0:T(128)}, u32[]{:S(2)}) copy-start(f32[128]{0:T(128)} %param.29) | copy-start | bytes 1540

commit v4 on v3

--- a/solution.py
+++ b/solution.py
@@ -253,11 +253,11 @@
     whole = gather(latent)
     whole, wanted = lax.optimization_barrier((whole, wanted))
     (offered,) = call(
-        offer, (export_rows, whole, *sender), [((n_y, offers, share), bf16)]
+        offer, (export_rows, whole, *sender), [((n_core * n_y, offers, share), bf16)]
     )
 
     offered, later = lax.optimization_barrier((offered, whole))
-    offered = lax.all_to_all(offered, "y", 0, 0).reshape(n_y * offers, share)
+    offered = lax.all_to_all(offered, ("core", "y"), 0, 0).reshape(-1, share)
     message, side = call(
         send,
         (later, *sender, node_w2, node_b2),
@@ -265,7 +265,6 @@
         flops=WEIGHT,
     )
     other = lax.ppermute(side, "sect", [(i, i ^ 1) for i in range(n_sect)])
-    offered = lax.all_gather(offered, "core", axis=0, tiled=True)
     (halo,) = call(
         select,
         (wanted, offered),
@@ -274,7 +273,7 @@
         limit=ROOM,
     )
 
-    halo, other, later = lax.optimization_barrier((halo, other, later))
+    halo, later = lax.optimization_barrier((halo, later))
     halo = lax.all_to_all(halo, "z", 0, 0)
     upper, pair = call(
         above,

time: 85.6 us -> 83.2 us (0.972)
  blocking collectives: 30 us -> 28.1 us
  waiting for transfers between devices: 10.4 us -> 9.03 us
    all_gather x1 -> x0, blocking collectives: 1.89 us -> none  [local(): offered = lax.all_gather(offered, 'core', axis=0, tiled=True)]
    all_to_all x1, waiting for transfers between devices: 6.85 us -> 5.39 us  [local(): halo = lax.all_to_all(halo, 'z', 0, 0)]
where the time goes in v4:
time: 83.2 us; the launch traced here: 82.5 us
  starting transfers between devices  29.1 us (35%)
  blocking collectives  28.1 us (34%)
  Pallas kernels  14.1 us (17%)
  waiting for transfers between devices  9.03 us (11%)
  local copies, waits for them, and re-layouts  2 us (2%)
    all_gather x4, blocking collectives, gather(): lax.all_gather(block, ('core', 'sect'), axis=0, axis_index_groups=groups,...  28.1 us
    pallas_call x6, Pallas kernels, call(): pl.pallas_call(kernel, out_shape=[jax.ShapeDtypeStruct(shape, kind) for s...  14.1 us
    all_to_all x1, starting transfers between devices, local(): lax.all_to_all(jnp.broadcast_to(slots[None], (n_z,) + slots.shape), 'z',...  10.3 us
    all_to_all x1, starting transfers between devices, local(): halo = lax.all_to_all(halo, 'z', 0, 0)  7.22 us
    all_to_all x1, starting transfers between devices, local(): offered = lax.all_to_all(offered, ('core', 'y'), 0, 0).reshape(-1, share)  7.22 us
    all_to_all x1, waiting for transfers between devices, local(): halo = lax.all_to_all(halo, 'z', 0, 0)  5.39 us
    all_to_all x1, waiting for transfers between devices, local(): offered = lax.all_to_all(offered, ('core', 'y'), 0, 0).reshape(-1, share)  3.63 us
    ppermute x1, starting transfers between devices, local(): lax.ppermute(pair, 'sect', [(i, n_sect - 1 - i) for i in range(n_sect)])  2.39 us
  transfers between devices with their start and end apart: 5, of which 2 were waited for; matrix products, arithmetic and copies ran while one was open for 0% of the time, Pallas kernels for 7%

profile of v4, /device:TPU:6, one launch (start us, length us, event | category | flops | bytes accessed | tf_op | source)
XLA Modules:
  0.0 82.5 jit_solution(17834157478330999876)
XLA Ops:
  0.0 1.3 %broadcast_in_dim.25 = s32[8,8,128]{2,1,0:T(8,128)} broadcast(s32[8,128]{1,0:T(8,128)} %bitcast.18), dimensions={1,2} | broadcast | bytes 36864 | tf_op jit(solution)/shard_map/broadcast_in_dim | solution.py:252
  1.3 10.3 %all-to-all-start = ((s32[8,8,128]{2,1,0:T(8,128)}), s32[8,8,128]{2,1,0:T(8,128)S(1)}, u32[]{:S(2)}, u32[]{:S(2)}) async-start(s32[8,8,128]{2,1,0:T(8,128)} %broadcast_in_dim.25), calls=%async_computation | async-start | bytes 65536 | tf_op jit(solution)/shard_map/all_to_all | solution.py:252
  11.6 5.8 %all-gather = bf16[1024,128]{1,0:T(8,128)(2,1)S(1)} all-gather(bf16[512,128]{1,0:T(8,128)(2,1)} %refs_8_.1), channel_id=2, replica_groups={{0,1},{2,3},{4,7},{5,6},{8,9},{10,11},{12,15},{13,14},{16,17},{18,19},{..., dimensions={0}, use_global_device_ids=true | all-gather | bytes 393216 | tf_op jit(solution)/shard_map/all_gather | solution.py:83
  17.5 8.4 %all_gather.20.refs_1_.refs_0_ = bf16[4,512,128]{2,1,0:T(8,128)(2,1)} all-gather(bf16[2,512,128]{2,1,0:T(8,128)(2,1)S(1)} %bitcast.17), channel_id=1, replica_groups={{0,3},{1,2},{4,5},{7,6},{8,11},{9,10},{12,13},{15,14},{16,19},{17,18},{..., dimensions={0}, use_global_device_ids=true | all-gather | bytes 786432 | tf_op jit(solution)/shard_map/all_gather | solution.py:83
  25.8 2.4 %offer.1 = bf16[16,32,128]{2,1,0:T(8,128)(2,1)} custom-call(s32[1,32]{1,0:T(1,128)} %refs_0_.3, bf16[4,512,128]{2,1,0:T(8,128)(2,1)} %all_gather.20.refs_1_.refs_0_, bf16[512,512]{1,0:T(8,128)(2,1)} %refs_1_.2, f32[1,512]{1,0:T(1,128)} %bitcast.19, bf16[512,128]{1,0:T(8,128)(2,1)} %refs_3_.2, f32[1,128]{1,0:T(1,128)} %bitcast.21), custom_call_target="tpu_custom_call" | custom-call | tf_op jit(solution)/shard_map/offer/pallas_call | solution.py:50
  28.3 7.2 %all-to-all-start.1 = ((bf16[16,32,128]{2,1,0:T(8,128)(2,1)}), bf16[16,32,128]{2,1,0:T(8,128)(2,1)S(1)}, u32[]{:S(2)}, u32[]{:S(2)}) async-start(bf16[16,32,128]{2,1,0:T(8,128)(2,1)} %offer.1), calls=%async_computation.1 | async-start | bytes 262144 | tf_op jit(solution)/shard_map/all_to_all | solution.py:260
  35.5 2.9 %send.1 = (bf16[512,128]{1,0:T(8,128)(2,1)}, bf16[528,128]{1,0:T(8,128)(2,1)}) custom-call(bf16[4,512,128]{2,1,0:T(8,128)(2,1)} %all_gather.20.refs_1_.refs_0_, bf16[512,512]{1,0:T(8,128)(2,1)} %refs_1_.2, f32[1,512]{1,0:T(1,128)} %bitcast.20, bf16[512,128]{1,0:T(8,128)(2,1)} %refs_3_.2, f32[1,128]{1,0:T(1,128)} %bitcast.22, bf16[512,128]{1,0:T(8,128)(2,1)} %refs_5_.2, ...), custom_call_target="tpu_custom_call" | custom-call | flops 10000000000 | tf_op jit(solution)/shard_map/send/pallas_call | solution.py:50
  38.4 1.9 %collective-permute-start = (bf16[528,128]{1,0:T(8,128)(2,1)}, bf16[528,128]{1,0:T(8,128)(2,1)S(1)}, u32[]{:S(2)}, u32[]{:S(2)}) collective-permute-start(bf16[528,128]{1,0:T(8,128)(2,1)} %get-tuple-element.24.refs_2_), channel_id=1, source_target_pairs={{0,1},{1,0},{2,3},{3,2},{4,5},{5,4},{6,7},{7,6},{8,9},{9,8},{10,11... | collective-permute-start | bytes 405512 | tf_op jit(solution)/shard_map/ppermute | solution.py:267
  40.3 3.6 %all-to-all-done.1 = bf16[16,32,128]{2,1,0:T(8,128)(2,1)S(1)} async-done(((bf16[16,32,128]{2,1,0:T(8,128)(2,1)}), bf16[16,32,128]{2,1,0:T(8,128)(2,1)S(1)}, u32[]{:S(2)}, u32[]{:S(2)}) %all-to-all-start.1) | async-done | bytes 131104 | tf_op jit(solution)/shard_map/all_to_all | solution.py:260
  44.0 1.4 %select.1 = bf16[8,128,128]{2,1,0:T(8,128)(2,1)} custom-call(s32[8,8,128]{2,1,0:T(8,128)S(1)} %all-to-all-done.refs_0_, bf16[512,128]{1,0:T(8,128)(2,1)S(1)} %bitcast.12), custom_call_target="tpu_custom_call" | custom-call | flops 20000000000 | tf_op jit(solution)/shard_map/select/pallas_call | solution.py:50
  45.4 7.2 %all-to-all-start.2 = ((bf16[8,128,128]{2,1,0:T(8,128)(2,1)}), bf16[8,128,128]{2,1,0:T(8,128)(2,1)S(1)}, u32[]{:S(2)}, u32[]{:S(2)}) async-start(bf16[8,128,128]{2,1,0:T(8,128)(2,1)} %select.1), calls=%async_computation.2 | async-start | bytes 524288 | tf_op jit(solution)/shard_map/all_to_all | solution.py:277
  52.6 0.0 copy-start.8
  52.6 0.0 copy-start.9
  52.6 0.6 copy-done.10
  53.3 2.8 %above.1 = (f32[512,512]{1,0:T(8,128)}, bf16[2,528,128]{2,1,0:T(8,128)(2,1)}) custom-call(bf16[4,512,128]{2,1,0:T(8,128)(2,1)} %all_gather.20.refs_1_.refs_0_, bf16[1024,512]{1,0:T(8,128)(2,1)} %refs_0_.5, bf16[528,128]{1,0:T(8,128)(2,1)} %get-tuple-element.24.refs_2_, bf16[528,128]{1,0:T(8,128)(2,1)} %copy-done.10), custom_call_target="tpu_custom_call" | custom-call | flops 10000000000 | tf_op jit(solution)/shard_map/above/pallas_call | solution.py:50
  56.1 2.4 %collective-permute-start.1 = (bf16[2,528,128]{2,1,0:T(8,128)(2,1)}, bf16[2,528,128]{2,1,0:T(8,128)(2,1)S(1)}, u32[]{:S(2)}, u32[]{:S(2)}) collective-permute-start(bf16[2,528,128]{2,1,0:T(8,128)(2,1)} %get-tuple-element.25.refs_6_), channel_id=1, source_target_pairs={{0,3},{1,2},{2,1},{3,0},{4,7},{5,6},{6,5},{7,4},{8,11},{9,10},{10,... | collective-permute-start | bytes 811016 | tf_op jit(solution)/shard_map/ppermute | solution.py:285
  58.5 5.4 %all-to-all-done.2.refs_2_ = bf16[8,128,128]{2,1,0:T(8,128)(2,1)S(1)} async-done(((bf16[8,128,128]{2,1,0:T(8,128)(2,1)}), bf16[8,128,128]{2,1,0:T(8,128)(2,1)S(1)}, u32[]{:S(2)}, u32[]{:S(2)}) %all-to-all-start.2) | async-done | bytes 262176 | tf_op jit(solution)/shard_map/all_to_all | solution.py:277
  63.9 0.0 copy-start.1
  63.9 0.0 copy-start.2
  63.9 0.0 copy-start.4
  64.0 1.8 %tiles.1 = bf16[512,128]{1,0:T(8,128)(2,1)S(1)} custom-call(s32[4,16]{1,0:T(4,128)S(1)} %copy-done.8, bf16[512,128]{1,0:T(8,128)(2,1)S(1)} %copy-done.9, bf16[8,128,128]{2,1,0:T(8,128)(2,1)S(1)} %all-to-all-done.2.refs_2_, bf16[4,16,128,128]{3,2,1,0:T(8,128)(2,1)S(1)} %copy-done.7, bf16[4,16,128,128]{3,2,1,0:T(8,128)(2,1)S(1)} %copy-done.7, ...), custom_call_target="tpu_custom_call" | custom-call | flops 20000000000 | tf_op jit(solution)/shard_map/tiles/pallas_call | solution.py:50
  65.8 5.6 %all-gather.1 = bf16[1024,128]{1,0:T(8,128)(2,1)S(1)} all-gather(bf16[512,128]{1,0:T(8,128)(2,1)S(1)} %tiles.1), channel_id=3, replica_groups={{0,1},{2,3},{4,7},{5,6},{8,9},{10,11},{12,15},{13,14},{16,17},{18,19},{..., dimensions={0}, use_global_device_ids=true | all-gather | bytes 393216 | tf_op jit(solution)/shard_map/all_gather | solution.py:83
  71.4 8.2 %all_gather.23.refs_2_.refs_4_ = bf16[4,512,128]{2,1,0:T(8,128)(2,1)S(1)} all-gather(bf16[2,512,128]{2,1,0:T(8,128)(2,1)S(1)} %bitcast.16), channel_id=1, replica_groups={{0,3},{1,2},{4,5},{7,6},{8,11},{9,10},{12,13},{15,14},{16,19},{17,18},{..., dimensions={0}, use_global_device_ids=true | all-gather | bytes 786432 | tf_op jit(solution)/shard_map/all_gather | solution.py:83
  79.7 2.8 %node.1 = bf16[512,128]{1,0:T(8,128)(2,1)} custom-call(bf16[1024,512]{1,0:T(8,128)(2,1)S(1)} %copy-done.1, f32[1,512]{1,0:T(1,128)S(1)} %bitcast.13, bf16[4,512,128]{2,1,0:T(8,128)(2,1)S(1)} %all_gather.23.refs_2_.refs_4_, f32[512,512]{1,0:T(8,128)S(1)} %copy-done, bf16[4,512,128]{2,1,0:T(8,128)(2,1)S(1)} %all_gather.23.refs_2_.refs_4_, ...), custom_call_target="tpu_custom_call" | custom-call | tf_op jit(solution)/shard_map/node/pallas_call | solution.py:50
  (19 shorter events, 0.0 us)
Async XLA Ops:
  1.3 24.5 %all-to-all-start = ((s32[8,8,128]{2,1,0:T(8,128)}), s32[8,8,128]{2,1,0:T(8,128)S(1)}, u32[]{:S(2)}, u32[]{:S(2)}) async-start(s32[8,8,128]{2,1,0:T(8,128)} %broadcast_in_dim.25), calls=%async_computation | async-start | bytes 65536 | tf_op jit(solution)/shard_map/all_to_all | solution.py:252
  28.3 15.7 %all-to-all-start.1 = ((bf16[16,32,128]{2,1,0:T(8,128)(2,1)}), bf16[16,32,128]{2,1,0:T(8,128)(2,1)S(1)}, u32[]{:S(2)}, u32[]{:S(2)}) async-start(bf16[16,32,128]{2,1,0:T(8,128)(2,1)} %offer.1), calls=%async_computation.1 | async-start | bytes 262144 | tf_op jit(solution)/shard_map/all_to_all | solution.py:260
  38.4 14.2 %collective-permute-start = (bf16[528,128]{1,0:T(8,128)(2,1)}, bf16[528,128]{1,0:T(8,128)(2,1)S(1)}, u32[]{:S(2)}, u32[]{:S(2)}) collective-permute-start(bf16[528,128]{1,0:T(8,128)(2,1)} %get-tuple-element.24.refs_2_), channel_id=1, source_target_pairs={{0,1},{1,0},{2,3},{3,2},{4,5},{5,4},{6,7},{7,6},{8,9},{9,8},{10,11... | collective-permute-start | bytes 405512 | tf_op jit(solution)/shard_map/ppermute | solution.py:267
  45.4 18.5 %all-to-all-start.2 = ((bf16[8,128,128]{2,1,0:T(8,128)(2,1)}), bf16[8,128,128]{2,1,0:T(8,128)(2,1)S(1)}, u32[]{:S(2)}, u32[]{:S(2)}) async-start(bf16[8,128,128]{2,1,0:T(8,128)(2,1)} %select.1), calls=%async_computation.2 | async-start | bytes 524288 | tf_op jit(solution)/shard_map/all_to_all | solution.py:277
  52.6 11.3 %copy-start.7 = (bf16[4,16,128,128]{3,2,1,0:T(8,128)(2,1)S(1)}, bf16[4,16,128,128]{3,2,1,0:T(8,128)(2,1)}, u32[]{:S(2)}) copy-start(bf16[4,16,128,128]{3,2,1,0:T(8,128)(2,1)} %refs_6_.1) | copy-start | bytes 6291460
  52.6 11.3 %copy-start.8 = (s32[4,16]{1,0:T(4,128)S(1)}, s32[4,16]{1,0:T(4,128)}, u32[]{:S(2)}) copy-start(s32[4,16]{1,0:T(4,128)} %refs_0_.4) | copy-start | bytes 772
  52.6 11.3 %copy-start.9 = (bf16[512,128]{1,0:T(8,128)(2,1)S(1)}, bf16[512,128]{1,0:T(8,128)(2,1)}, u32[]{:S(2)}) copy-start(bf16[512,128]{1,0:T(8,128)(2,1)} %get-tuple-element.19.refs_1_) | copy-start | bytes 393220
  52.6 0.6 copy-start.10
  56.1 15.3 %collective-permute-start.1 = (bf16[2,528,128]{2,1,0:T(8,128)(2,1)}, bf16[2,528,128]{2,1,0:T(8,128)(2,1)S(1)}, u32[]{:S(2)}, u32[]{:S(2)}) collective-permute-start(bf16[2,528,128]{2,1,0:T(8,128)(2,1)} %get-tuple-element.25.refs_6_), channel_id=1, source_target_pairs={{0,3},{1,2},{2,1},{3,0},{4,7},{5,6},{6,5},{7,4},{8,11},{9,10},{10,... | collective-permute-start | bytes 811016 | tf_op jit(solution)/shard_map/ppermute | solution.py:285
  63.9 15.8 %copy-start = (f32[512,512]{1,0:T(8,128)S(1)}, f32[512,512]{1,0:T(8,128)}, u32[]{:S(2)}) copy-start(f32[512,512]{1,0:T(8,128)} %get-tuple-element.27.refs_3_.refs_5_) | copy-start | bytes 3145732
  63.9 15.8 %copy-start.1 = (bf16[1024,512]{1,0:T(8,128)(2,1)S(1)}, bf16[1024,512]{1,0:T(8,128)(2,1)}, u32[]{:S(2)}) copy-start(bf16[1024,512]{1,0:T(8,128)(2,1)} %refs_0_.5) | copy-start | bytes 3145732
  63.9 15.8 %copy-start.2 = (bf16[512,128]{1,0:T(8,128)(2,1)S(1)}, bf16[512,128]{1,0:T(8,128)(2,1)}, u32[]{:S(2)}) copy-start(bf16[512,128]{1,0:T(8,128)(2,1)} %refs_8_.1) | copy-start | bytes 393220
  63.9 15.8 %copy-start.3 = (bf16[2,528,128]{2,1,0:T(8,128)(2,1)S(1)}, bf16[2,528,128]{2,1,0:T(8,128)(2,1)}, u32[]{:S(2)}) copy-start(bf16[2,528,128]{2,1,0:T(8,128)(2,1)} %get-tuple-element.25.refs_6_) | copy-start | bytes 811012
  63.9 15.8 %copy-start.4 = (f32[512]{0:T(512)S(1)}, f32[512]{0:T(512)}, u32[]{:S(2)}) copy-start(f32[512]{0:T(512)} %param.25) | copy-start | bytes 6148
  63.9 15.8 %copy-start.5 = (f32[128]{0:T(128)S(1)}, f32[128]{0:T(128)}, u32[]{:S(2)}) copy-start(f32[128]{0:T(128)} %param.28) | copy-start | bytes 1540
  63.9 15.8 %copy-start.6 = (f32[128]{0:T(128)S(1)}, f32[128]{0:T(128)}, u32[]{:S(2)}) copy-start(f32[128]{0:T(128)} %param.29) | copy-start | bytes 1540

commit v5 on v4

--- a/solution.py
+++ b/solution.py
@@ -16,29 +16,29 @@
 bf16, f32, i32 = jnp.bfloat16, jnp.float32, jnp.int32
 
 
-def call(body, operands, outs, scratch=(), scalars=(), part={}, flops=0, moved=0, limit=LIMIT):
+def call(body, operands, outs, scratch=(), scalars=(), part={}, flops=0, limit=LIMIT):
     count = len(operands)
-    space = [pltpu.SMEM if i in scalars else pltpu.VMEM for i in range(count)]
+    moved = [i for i in range(count) if limit == LIMIT or i in scalars]
+    vmem, hbm = (pl.BlockSpec(memory_space=space) for space in (pltpu.VMEM, pltpu.HBM))
 
     def kernel(*refs):
         sources, rest = refs[:count], refs[count:]
-        results, held, rest = rest[: len(outs)], rest[len(outs) :][:count], rest[len(outs) + count :]
-        sems, extra = rest[-1], rest[:-1]
-        copies = [
-            pltpu.make_async_copy(
-                source.at[part[i][0]] if i in part else source, target, sems.at[i]
-            )
-            for i, (source, target) in enumerate(zip(sources, held))
-        ]
-        for copy in copies:
+        results, rest = rest[: len(outs)], rest[len(outs) :]
+        held, extra, sems = rest[: len(moved)], rest[len(moved) :], None
+        if moved:
+            extra, sems = extra[:-1], extra[-1]
+        views = [ref.at[part[i][0]] if i in part else ref for i, ref in enumerate(sources)]
+        copies = {
+            i: pltpu.make_async_copy(views[i], held[n], sems.at[n]) for n, i in enumerate(moved)
+        }
+        for copy in copies.values():
             copy.start()
 
         def ready(i):
             def get():
-                if copies[i] is not None:
-                    copies[i].wait()
-                    copies[i] = None
-                return held[i]
+                if i in copies:
+                    copies.pop(i).wait()
+                return held[moved.index(i)] if i in moved else views[i]
 
             return get
 
@@ -47,19 +47,23 @@
         for get in gets:
             get()
 
+    scratch = list(scratch)
+    if moved:
+        scratch.append(pltpu.SemaphoreType.DMA((len(moved),)))
     return pl.pallas_call(
         kernel,
         out_shape=[jax.ShapeDtypeStruct(shape, kind) for shape, kind in outs],
-        in_specs=[pl.BlockSpec(memory_space=pltpu.HBM)] * count,
-        out_specs=[pl.BlockSpec(memory_space=pltpu.VMEM)] * len(outs),
+        in_specs=[hbm if i in moved else vmem for i in range(count)],
+        out_specs=[vmem] * len(outs),
         scratch_shapes=[
-            kind(part[i][1] if i in part else v.shape, v.dtype)
-            for i, (kind, v) in enumerate(zip(space, operands))
+            (pltpu.SMEM if i in scalars else pltpu.VMEM)(
+                part[i][1] if i in part else operands[i].shape, operands[i].dtype
+            )
+            for i in moved
         ]
-        + list(scratch)
-        + [pltpu.SemaphoreType.DMA((count,))],
+        + scratch,
         compiler_params=pltpu.CompilerParams(vmem_limit_bytes=limit),
-        cost_estimate=pl.CostEstimate(flops=flops, bytes_accessed=moved, transcendentals=0),
+        cost_estimate=pl.CostEstimate(flops=flops, bytes_accessed=0, transcendentals=0),
         name=body.__name__,
     )(*operands)
 
@@ -89,6 +93,11 @@
 def ordered(whole):
     core = lax.axis_index("core")
     return [whole.at[0], whole.at[1 + core], whole.at[2 + core], whole.at[3 - 2 * core]]
+
+
+def spread(slots, out):
+    for peer in range(out.shape[0]):
+        out[peer] = slots()[...]
 
 
 def offer(export, latent, w1, b1, w2, b2, out):
@@ -249,11 +258,14 @@
     sender = (send_w1, send_b1, send_w2, send_b2)
 
     slots = jnp.swapaxes(halo_slots[0], 0, 1)
-    wanted = lax.all_to_all(jnp.broadcast_to(slots[None], (n_z,) + slots.shape), "z", 0, 0)
+    (wanted,) = call(
+        spread, (slots,), [((n_z,) + slots.shape, i32)], flops=WEIGHT, limit=ROOM
+    )
+    wanted = lax.all_to_all(wanted, "z", 0, 0)
     whole = gather(latent)
     whole, wanted = lax.optimization_barrier((whole, wanted))
     (offered,) = call(
-        offer, (export_rows, whole, *sender), [((n_core * n_y, offers, share), bf16)]
+        offer, (export_rows, whole, *sender), [((n_core * n_y, offers, share), bf16)], flops=WEIGHT, limit=ROOM
     )
 
     offered, later = lax.optimization_barrier((offered, whole))
@@ -263,6 +275,7 @@
         (later, *sender, node_w2, node_b2),
         [((rows, share), bf16), ((width + TAIL, share), bf16)],
         flops=WEIGHT,
+        limit=ROOM,
     )
     other = lax.ppermute(side, "sect", [(i, i ^ 1) for i in range(n_sect)])
     (halo,) = call(

time: 83.2 us -> 80 us (0.962)
  Pallas kernels: 14.1 us -> 9.67 us
  waiting for transfers between devices: 9.03 us -> 11.1 us
    pallas_call x6 -> x7, Pallas kernels: 14.1 us -> 9.67 us  [call(): pl.pallas_call(kernel, out_shape=[jax.ShapeDtypeStruct(shape, kind) for s...]
    all_to_all x1, waiting for transfers between devices: 3.63 us -> 5.69 us  [local(): offered = lax.all_to_all(offered, ('core', 'y'), 0, 0).reshape(-1, share)]
    broadcast_in_dim x1 -> x0, local copies, waits for them, and re-layouts: 1.3 us -> none  [local(): jnp.broadcast_to(slots[None], (n_z,) + slots.shape)]
where the time goes in v5:
time: 80 us; the launch traced here: 79.3 us
  starting transfers between devices  29 us (36%)
  blocking collectives  27.8 us (35%)
  waiting for transfers between devices  11.1 us (14%)
  Pallas kernels  9.67 us (12%)
  local copies, waits for them, and re-layouts  1.42 us (2%)
    all_gather x4, blocking collectives, gather(): lax.all_gather(block, ('core', 'sect'), axis=0, axis_index_groups=groups,...  27.8 us
    all_to_all x1, starting transfers between devices, local(): wanted = lax.all_to_all(wanted, 'z', 0, 0)  10.3 us
    pallas_call x7, Pallas kernels, call(): pl.pallas_call(kernel, out_shape=[jax.ShapeDtypeStruct(shape, kind) for s...  9.67 us
    all_to_all x1, starting transfers between devices, local(): offered = lax.all_to_all(offered, ('core', 'y'), 0, 0).reshape(-1, share)  7.21 us
    all_to_all x1, starting transfers between devices, local(): halo = lax.all_to_all(halo, 'z', 0, 0)  7.19 us
    all_to_all x1, waiting for transfers between devices, local(): offered = lax.all_to_all(offered, ('core', 'y'), 0, 0).reshape(-1, share)  5.69 us
    all_to_all x1, waiting for transfers between devices, local(): halo = lax.all_to_all(halo, 'z', 0, 0)  5.42 us
    ppermute x1, starting transfers between devices, local(): lax.ppermute(pair, 'sect', [(i, n_sect - 1 - i) for i in range(n_sect)])  2.39 us
  transfers between devices with their start and end apart: 5, of which 2 were waited for; matrix products, arithmetic and copies ran while one was open for 0% of the time, Pallas kernels for 7%

profile of v5, /device:TPU:6, one launch (start us, length us, event | category | flops | bytes accessed | tf_op | source)
XLA Modules:
  0.0 79.3 jit_solution(12133380830182698875)
XLA Ops:
  0.0 0.7 copy-done.13
  0.7 0.6 spread.1
  1.3 10.3 %all-to-all-start = ((s32[8,8,128]{2,1,0:T(8,128)}), s32[8,8,128]{2,1,0:T(8,128)S(1)}, u32[]{:S(2)}, u32[]{:S(2)}) async-start(s32[8,8,128]{2,1,0:T(8,128)} %spread.1), calls=%async_computation | async-start | bytes 65536 | tf_op jit(solution)/shard_map/all_to_all | solution.py:264
  11.7 5.6 %all-gather = bf16[1024,128]{1,0:T(8,128)(2,1)S(1)} all-gather(bf16[512,128]{1,0:T(8,128)(2,1)S(1)} %copy-done.2), channel_id=2, replica_groups={{0,1},{2,3},{4,7},{5,6},{8,9},{10,11},{12,15},{13,14},{16,17},{18,19},{..., dimensions={0}, use_global_device_ids=true | all-gather | bytes 393216 | tf_op jit(solution)/shard_map/all_gather | solution.py:87
  17.3 8.2 %all_gather.20.refs_1_.refs_0_ = bf16[4,512,128]{2,1,0:T(8,128)(2,1)S(1)} all-gather(bf16[2,512,128]{2,1,0:T(8,128)(2,1)S(1)} %bitcast.23), channel_id=1, replica_groups={{0,3},{1,2},{4,5},{7,6},{8,11},{9,10},{12,13},{15,14},{16,19},{17,18},{..., dimensions={0}, use_global_device_ids=true | all-gather | bytes 786432 | tf_op jit(solution)/shard_map/all_gather | solution.py:87
  25.6 0.0 copy-start.18
  25.6 1.2 %offer.1 = bf16[16,32,128]{2,1,0:T(8,128)(2,1)} custom-call(s32[1,32]{1,0:T(1,128)S(1)} %copy-done.16, bf16[4,512,128]{2,1,0:T(8,128)(2,1)S(1)} %all_gather.20.refs_1_.refs_0_, bf16[512,512]{1,0:T(8,128)(2,1)S(1)} %copy-done.9, f32[1,512]{1,0:T(1,128)S(1)} %bitcast.17, bf16[512,128]{1,0:T(8,128)(2,1)S(1)} %copy-done.11, f32[1,128]{1,0:T(1,128)S(1)} %bitcast.19), custom_call_target="tpu_custom_call" | custom-call | flops 10000000000 | tf_op jit(solution)/shard_map/offer/pallas_call | solution.py:53
  26.8 7.2 %all-to-all-start.1 = ((bf16[16,32,128]{2,1,0:T(8,128)(2,1)}), bf16[16,32,128]{2,1,0:T(8,128)(2,1)S(1)}, u32[]{:S(2)}, u32[]{:S(2)}) async-start(bf16[16,32,128]{2,1,0:T(8,128)(2,1)} %offer.1), calls=%async_computation.1 | async-start | bytes 262144 | tf_op jit(solution)/shard_map/all_to_all | solution.py:272
  34.1 0.8 %send.1 = (bf16[512,128]{1,0:T(8,128)(2,1)S(1)}, bf16[528,128]{1,0:T(8,128)(2,1)S(1)}) custom-call(bf16[4,512,128]{2,1,0:T(8,128)(2,1)S(1)} %all_gather.20.refs_1_.refs_0_, bf16[512,512]{1,0:T(8,128)(2,1)S(1)} %copy-done.9, f32[1,512]{1,0:T(1,128)S(1)} %bitcast.18, bf16[512,128]{1,0:T(8,128)(2,1)S(1)} %copy-done.11, f32[1,128]{1,0:T(1,128)S(1)} %bitcast.20, ...), custom_call_target="tpu_custom_call" | custom-call | flops 10000000000 | tf_op jit(solution)/shard_map/send/pallas_call | solution.py:53
  34.9 1.9 %collective-permute-start = (bf16[528,128]{1,0:T(8,128)(2,1)S(1)}, bf16[528,128]{1,0:T(8,128)(2,1)S(1)}, u32[]{:S(2)}, u32[]{:S(2)}) collective-permute-start(bf16[528,128]{1,0:T(8,128)(2,1)S(1)} %get-tuple-element.24.refs_2_), channel_id=1, source_target_pairs={{0,1},{1,0},{2,3},{3,2},{4,5},{5,4},{6,7},{7,6},{8,9},{9,8},{10,11... | collective-permute-start | bytes 405512 | tf_op jit(solution)/shard_map/ppermute | solution.py:280
  36.8 5.7 %all-to-all-done.1 = bf16[16,32,128]{2,1,0:T(8,128)(2,1)S(1)} async-done(((bf16[16,32,128]{2,1,0:T(8,128)(2,1)}), bf16[16,32,128]{2,1,0:T(8,128)(2,1)S(1)}, u32[]{:S(2)}, u32[]{:S(2)}) %all-to-all-start.1) | async-done | bytes 131104 | tf_op jit(solution)/shard_map/all_to_all | solution.py:272
  42.5 1.2 %select.1 = bf16[8,128,128]{2,1,0:T(8,128)(2,1)} custom-call(s32[8,8,128]{2,1,0:T(8,128)S(1)} %all-to-all-done.refs_0_, bf16[512,128]{1,0:T(8,128)(2,1)S(1)} %bitcast.12), custom_call_target="tpu_custom_call" | custom-call | flops 20000000000 | tf_op jit(solution)/shard_map/select/pallas_call | solution.py:53
  43.7 7.2 %all-to-all-start.2 = ((bf16[8,128,128]{2,1,0:T(8,128)(2,1)}), bf16[8,128,128]{2,1,0:T(8,128)(2,1)S(1)}, u32[]{:S(2)}, u32[]{:S(2)}) async-start(bf16[8,128,128]{2,1,0:T(8,128)(2,1)} %select.1), calls=%async_computation.2 | async-start | bytes 524288 | tf_op jit(solution)/shard_map/all_to_all | solution.py:290
  50.9 0.0 copy-start.15
  50.9 0.6 copy-done.19
  51.6 2.8 %above.1 = (f32[512,512]{1,0:T(8,128)}, bf16[2,528,128]{2,1,0:T(8,128)(2,1)}) custom-call(bf16[4,512,128]{2,1,0:T(8,128)(2,1)} %copy-done.3, bf16[1024,512]{1,0:T(8,128)(2,1)} %refs_0_.5, bf16[528,128]{1,0:T(8,128)(2,1)} %copy-done.10, bf16[528,128]{1,0:T(8,128)(2,1)} %copy-done.19), custom_call_target="tpu_custom_call" | custom-call | flops 10000000000 | tf_op jit(solution)/shard_map/above/pallas_call | solution.py:53
  54.4 2.4 %collective-permute-start.1 = (bf16[2,528,128]{2,1,0:T(8,128)(2,1)}, bf16[2,528,128]{2,1,0:T(8,128)(2,1)S(1)}, u32[]{:S(2)}, u32[]{:S(2)}) collective-permute-start(bf16[2,528,128]{2,1,0:T(8,128)(2,1)} %get-tuple-element.25.refs_6_), channel_id=1, source_target_pairs={{0,3},{1,2},{2,1},{3,0},{4,7},{5,6},{6,5},{7,4},{8,11},{9,10},{10,... | collective-permute-start | bytes 811016 | tf_op jit(solution)/shard_map/ppermute | solution.py:298
  56.8 5.4 %all-to-all-done.2.refs_2_ = bf16[8,128,128]{2,1,0:T(8,128)(2,1)S(1)} async-done(((bf16[8,128,128]{2,1,0:T(8,128)(2,1)}), bf16[8,128,128]{2,1,0:T(8,128)(2,1)S(1)}, u32[]{:S(2)}, u32[]{:S(2)}) %all-to-all-start.2) | async-done | bytes 262176 | tf_op jit(solution)/shard_map/all_to_all | solution.py:290
  62.2 0.0 copy-start.5
  62.2 0.0 copy-start.6
  62.2 1.3 %tiles.1 = bf16[512,128]{1,0:T(8,128)(2,1)S(1)} custom-call(s32[4,16]{1,0:T(4,128)S(1)} %copy-done.15, bf16[512,128]{1,0:T(8,128)(2,1)S(1)} %get-tuple-element.19.refs_1_, bf16[8,128,128]{2,1,0:T(8,128)(2,1)S(1)} %all-to-all-done.2.refs_2_, bf16[4,16,128,128]{3,2,1,0:T(8,128)(2,1)S(1)} %copy-done.8, bf16[4,16,128,128]{3,2,1,0:T(8,128)(2,1)S(1)} %copy-done.8, ...), custom_call_target="tpu_custom_call" | custom-call | flops 20000000000 | tf_op jit(solution)/shard_map/tiles/pallas_call | solution.py:53
  63.6 5.6 %all-gather.1 = bf16[1024,128]{1,0:T(8,128)(2,1)S(1)} all-gather(bf16[512,128]{1,0:T(8,128)(2,1)S(1)} %tiles.1), channel_id=3, replica_groups={{0,1},{2,3},{4,7},{5,6},{8,9},{10,11},{12,15},{13,14},{16,17},{18,19},{..., dimensions={0}, use_global_device_ids=true | all-gather | bytes 393216 | tf_op jit(solution)/shard_map/all_gather | solution.py:87
  69.2 8.2 %all_gather.23.refs_2_.refs_4_ = bf16[4,512,128]{2,1,0:T(8,128)(2,1)S(1)} all-gather(bf16[2,512,128]{2,1,0:T(8,128)(2,1)S(1)} %bitcast.22), channel_id=1, replica_groups={{0,3},{1,2},{4,5},{7,6},{8,11},{9,10},{12,13},{15,14},{16,19},{17,18},{..., dimensions={0}, use_global_device_ids=true | all-gather | bytes 786432 | tf_op jit(solution)/shard_map/all_gather | solution.py:87
  77.5 1.8 %node.1 = bf16[512,128]{1,0:T(8,128)(2,1)} custom-call(bf16[1024,512]{1,0:T(8,128)(2,1)S(1)} %copy-done.1, f32[1,512]{1,0:T(1,128)S(1)} %bitcast.13, bf16[4,512,128]{2,1,0:T(8,128)(2,1)S(1)} %all_gather.23.refs_2_.refs_4_, f32[512,512]{1,0:T(8,128)S(1)} %copy-done, bf16[4,512,128]{2,1,0:T(8,128)(2,1)S(1)} %all_gather.23.refs_2_.refs_4_, ...), custom_call_target="tpu_custom_call" | custom-call | tf_op jit(solution)/shard_map/node/pallas_call | solution.py:53
  (37 shorter events, 0.1 us)
Async XLA Ops:
  0.0 0.7 copy-start.13
  0.7 11.0 %copy-start.2 = (bf16[512,128]{1,0:T(8,128)(2,1)S(1)}, bf16[512,128]{1,0:T(8,128)(2,1)}, u32[]{:S(2)}) copy-start(bf16[512,128]{1,0:T(8,128)(2,1)} %refs_8_.1) | copy-start | bytes 393220
  0.7 24.9 %copy-start.9 = (bf16[512,512]{1,0:T(8,128)(2,1)S(1)}, bf16[512,512]{1,0:T(8,128)(2,1)}, u32[]{:S(2)}) copy-start(bf16[512,512]{1,0:T(8,128)(2,1)} %refs_1_.2) | copy-start | bytes 1572868
  0.7 24.9 %copy-start.11 = (bf16[512,128]{1,0:T(8,128)(2,1)S(1)}, bf16[512,128]{1,0:T(8,128)(2,1)}, u32[]{:S(2)}) copy-start(bf16[512,128]{1,0:T(8,128)(2,1)} %refs_3_.2) | copy-start | bytes 393220
  0.7 24.9 %copy-start.14 = (f32[512]{0:T(512)S(1)}, f32[512]{0:T(512)}, u32[]{:S(2)}) copy-start(f32[512]{0:T(512)} %param.21) | copy-start | bytes 6148
  0.7 24.9 %copy-start.16 = (s32[1,32]{1,0:T(1,128)S(1)}, s32[1,32]{1,0:T(1,128)}, u32[]{:S(2)}) copy-start(s32[1,32]{1,0:T(1,128)} %refs_0_.3) | copy-start | bytes 388
  0.7 24.9 %copy-start.17 = (f32[128]{0:T(128)S(1)}, f32[128]{0:T(128)}, u32[]{:S(2)}) copy-start(f32[128]{0:T(128)} %param.23) | copy-start | bytes 1540
  1.3 24.2 %all-to-all-start = ((s32[8,8,128]{2,1,0:T(8,128)}), s32[8,8,128]{2,1,0:T(8,128)S(1)}, u32[]{:S(2)}, u32[]{:S(2)}) async-start(s32[8,8,128]{2,1,0:T(8,128)} %spread.1), calls=%async_computation | async-start | bytes 65536 | tf_op jit(solution)/shard_map/all_to_all | solution.py:264
  25.6 8.5 %copy-start.3 = (bf16[4,512,128]{2,1,0:T(8,128)(2,1)}, bf16[4,512,128]{2,1,0:T(8,128)(2,1)S(1)}, u32[]{:S(2)}) copy-start(bf16[4,512,128]{2,1,0:T(8,128)(2,1)S(1)} %all_gather.20.refs_1_.refs_0_) | copy-start | bytes 1572868
  25.6 8.5 %copy-start.12 = (bf16[512,128]{1,0:T(8,128)(2,1)S(1)}, bf16[512,128]{1,0:T(8,128)(2,1)}, u32[]{:S(2)}) copy-start(bf16[512,128]{1,0:T(8,128)(2,1)} %refs_5_.2) | copy-start | bytes 393220
  25.6 8.5 %copy-start.18 = (bf16[128]{0:T(256)(128)(2,1)S(1)}, bf16[128]{0:T(256)(128)(2,1)}, u32[]{:S(2)}) copy-start(bf16[128]{0:T(256)(128)(2,1)} %param.27) | copy-start | bytes 772
  26.8 15.7 %all-to-all-start.1 = ((bf16[16,32,128]{2,1,0:T(8,128)(2,1)}), bf16[16,32,128]{2,1,0:T(8,128)(2,1)S(1)}, u32[]{:S(2)}, u32[]{:S(2)}) async-start(bf16[16,32,128]{2,1,0:T(8,128)(2,1)} %offer.1), calls=%async_computation.1 | async-start | bytes 262144 | tf_op jit(solution)/shard_map/all_to_all | solution.py:272
  34.9 8.8 %copy-start.10 = (bf16[528,128]{1,0:T(8,128)(2,1)}, bf16[528,128]{1,0:T(8,128)(2,1)S(1)}, u32[]{:S(2)}) copy-start(bf16[528,128]{1,0:T(8,128)(2,1)S(1)} %get-tuple-element.24.refs_2_) | copy-start | bytes 405508
  34.9 16.0 %collective-permute-start = (bf16[528,128]{1,0:T(8,128)(2,1)S(1)}, bf16[528,128]{1,0:T(8,128)(2,1)S(1)}, u32[]{:S(2)}, u32[]{:S(2)}) collective-permute-start(bf16[528,128]{1,0:T(8,128)(2,1)S(1)} %get-tuple-element.24.refs_2_), channel_id=1, source_target_pairs={{0,1},{1,0},{2,3},{3,2},{4,5},{5,4},{6,7},{7,6},{8,9},{9,8},{10,11... | collective-permute-start | bytes 405512 | tf_op jit(solution)/shard_map/ppermute | solution.py:280
  43.7 18.5 %all-to-all-start.2 = ((bf16[8,128,128]{2,1,0:T(8,128)(2,1)}), bf16[8,128,128]{2,1,0:T(8,128)(2,1)S(1)}, u32[]{:S(2)}, u32[]{:S(2)}) async-start(bf16[8,128,128]{2,1,0:T(8,128)(2,1)} %select.1), calls=%async_computation.2 | async-start | bytes 524288 | tf_op jit(solution)/shard_map/all_to_all | solution.py:290
  50.9 11.3 %copy-start.8 = (bf16[4,16,128,128]{3,2,1,0:T(8,128)(2,1)S(1)}, bf16[4,16,128,128]{3,2,1,0:T(8,128)(2,1)}, u32[]{:S(2)}) copy-start(bf16[4,16,128,128]{3,2,1,0:T(8,128)(2,1)} %refs_6_.1) | copy-start | bytes 6291460
  50.9 11.3 %copy-start.15 = (s32[4,16]{1,0:T(4,128)S(1)}, s32[4,16]{1,0:T(4,128)}, u32[]{:S(2)}) copy-start(s32[4,16]{1,0:T(4,128)} %refs_0_.4) | copy-start | bytes 772
  54.4 14.8 %collective-permute-start.1 = (bf16[2,528,128]{2,1,0:T(8,128)(2,1)}, bf16[2,528,128]{2,1,0:T(8,128)(2,1)S(1)}, u32[]{:S(2)}, u32[]{:S(2)}) collective-permute-start(bf16[2,528,128]{2,1,0:T(8,128)(2,1)} %get-tuple-element.25.refs_6_), channel_id=1, source_target_pairs={{0,3},{1,2},{2,1},{3,0},{4,7},{5,6},{6,5},{7,4},{8,11},{9,10},{10,... | collective-permute-start | bytes 811016 | tf_op jit(solution)/shard_map/ppermute | solution.py:298
  62.2 15.3 %copy-start = (f32[512,512]{1,0:T(8,128)S(1)}, f32[512,512]{1,0:T(8,128)}, u32[]{:S(2)}) copy-start(f32[512,512]{1,0:T(8,128)} %get-tuple-element.27.refs_3_.refs_5_) | copy-start | bytes 3145732
  62.2 15.3 %copy-start.1 = (bf16[1024,512]{1,0:T(8,128)(2,1)S(1)}, bf16[1024,512]{1,0:T(8,128)(2,1)}, u32[]{:S(2)}) copy-start(bf16[1024,512]{1,0:T(8,128)(2,1)} %refs_0_.5) | copy-start | bytes 3145732
  62.2 15.3 %copy-start.4 = (bf16[2,528,128]{2,1,0:T(8,128)(2,1)S(1)}, bf16[2,528,128]{2,1,0:T(8,128)(2,1)}, u32[]{:S(2)}) copy-start(bf16[2,528,128]{2,1,0:T(8,128)(2,1)} %get-tuple-element.25.refs_6_) | copy-start | bytes 811012
  62.2 15.2 %copy-start.5 = (f32[512]{0:T(512)S(1)}, f32[512]{0:T(512)}, u32[]{:S(2)}) copy-start(f32[512]{0:T(512)} %param.25) | copy-start | bytes 6148
  62.2 15.2 %copy-start.6 = (f32[128]{0:T(128)S(1)}, f32[128]{0:T(128)}, u32[]{:S(2)}) copy-start(f32[128]{0:T(128)} %param.28) | copy-start | bytes 1540
  62.2 15.2 %copy-start.7 = (f32[128]{0:T(128)S(1)}, f32[128]{0:T(128)}, u32[]{:S(2)}) copy-start(f32[128]{0:T(128)} %param.29) | copy-start | bytes 1540
  (1 other events, 0.7 us)

commit v6 on v5

--- a/solution.py
+++ b/solution.py
@@ -77,17 +77,15 @@
     return half + half * jnp.tanh(half)
 
 
-def gather(block, beside=None):
+def gather(block):
     near, far = [[0, 1], [2, 3]], [[0, 3], [1, 2]]
     turned = [[0, 1], [3, 2]]
     for first, second in ((near, far), (far, turned)):
         groups = first + [[4 + i for i in group] for group in second]
-        if block.ndim > 2 and beside is not None:
-            block, beside = lax.optimization_barrier((block, beside))
         block = lax.all_gather(
             block, ("core", "sect"), axis=0, axis_index_groups=groups, tiled=block.ndim > 2
         )
-    return block if beside is None else (block, beside)
+    return block
 
 
 def ordered(whole):
@@ -166,7 +164,7 @@
     side[pl.ds(width, TAIL), :] = jnp.broadcast_to(row, (TAIL, row.shape[1])).astype(bf16)
 
 
-def above(latent, weight, side0, side1, upper, pair):
+def above(latent, weight, upper):
     rows = latent().shape[1]
     blocks = ordered(latent())
     step = rows // 2
@@ -174,8 +172,6 @@
         at = pl.ds(r, step)
         x = jnp.concatenate([block[at, :] for block in blocks], 1)
         upper[at, :] = matmul(x, weight()[...])
-    pair[0] = side0()[...]
-    pair[1] = side1()[...]
 
 
 def tiles(source, message, halo, *rest):
@@ -198,11 +194,13 @@
             left = jnp.concatenate([block()[k + g] for g in range(group)], 1)
             right = jnp.concatenate([extended[src[b, k + g]] for g in range(group)], 0)
             total = total + matmul(left, right)
-        out[pl.ds(b * tile, tile), :] = total.astype(bf16)
+        total = total.astype(bf16)
+        for peer in range(out.shape[0]):
+            out[peer, pl.ds(b * tile, tile), :] = total
 
 
 def node(lower_w, b1, *rest):
-    *chunks, pair0, pair1, latent, gain, bias, out = rest
+    *chunks, side0, side1, side2, side3, latent, gain, bias, out = rest
     sides = []
     r = 0
     for aggregate, upper in zip(chunks[::2], chunks[1::2]):
@@ -210,10 +208,10 @@
         width = share * parts
         at = pl.ds(r, step)
         r += step
-        x = jnp.concatenate([part[...] for part in ordered(aggregate())], 1)
+        x = jnp.concatenate([aggregate()[p] for p in range(parts)], 1)
         hidden = silu(upper()[...] + matmul(x, lower_w()[...]) + b1()[...]).astype(bf16)
         if not sides:
-            sides = [pair()[p] for pair in (pair0, pair1) for p in range(2)]
+            sides = [side()[...] for side in (side0, side1, side2, side3)]
             w2 = jnp.concatenate([side[:width] for side in sides], 1)
             b2 = jnp.concatenate([side[width : width + 1] for side in sides], 1).astype(f32)
         every = matmul(hidden, w2) + b2
@@ -277,7 +275,12 @@
         flops=WEIGHT,
         limit=ROOM,
     )
-    other = lax.ppermute(side, "sect", [(i, i ^ 1) for i in range(n_sect)])
+    near, far = [i ^ 1 for i in range(n_sect)], [n_sect - 1 - i for i in range(n_sect)]
+    first, second = (
+        [(c * n_sect + i, c * n_sect + j) for c, to in enumerate(order) for i, j in enumerate(to)]
+        for order in ((near, far), (far, near))
+    )
+    sides = [side] + [lax.ppermute(side, ("core", "sect"), to) for to in (first, second)]
     (halo,) = call(
         select,
         (wanted, offered),
@@ -288,27 +291,30 @@
 
     halo, later = lax.optimization_barrier((halo, later))
     halo = lax.all_to_all(halo, "z", 0, 0)
-    upper, pair = call(
+    later, *sides[1:] = lax.optimization_barrier((later, *sides[1:]))
+    (upper,) = call(
         above,
-        (later, node_w1, side, other),
-        [((rows, width), f32), ((2, width + TAIL, share), bf16)],
+        (later, node_w1),
+        [((rows, width), f32)],
         part={1: (pl.ds(0, width), (width, width))},
         flops=WEIGHT,
     )
-    others = lax.ppermute(pair, "sect", [(i, n_sect - 1 - i) for i in range(n_sect)])
+    passed, upper = lax.optimization_barrier((sides[1], upper))
+    others = lax.ppermute(passed, ("core", "sect"), second)
 
     blocks, terms = tile_src.shape
     (aggregate,) = call(
         tiles,
         (tile_src, message, halo) + (tile_weight,) * blocks,
-        [((rows, share), bf16)],
+        [((n_sect, rows, share), bf16)],
         [pltpu.VMEM((rows // tile + n_y, tile, share), bf16)],
         scalars=(0,),
         part={3 + b: (b, (terms, tile, tile)) for b in range(blocks)},
         limit=ROOM,
         flops=2 * WEIGHT,
     )
-    aggregate, others = gather(aggregate, others)
+    aggregate, others = lax.optimization_barrier((aggregate, others))
+    aggregate = lax.all_to_all(aggregate, "sect", 0, 0)
 
     step = rows // 2
     part = {0: (pl.ds(width, width), (width, width))}
@@ -320,7 +326,7 @@
         node,
         (node_w1, node_b1)
         + (aggregate, upper) * 2
-        + (pair, others, latent, ln_gain, ln_bias),
+        + (*sides, others, latent, ln_gain, ln_bias),
         [((rows, share), bf16)],
         part=part,
         limit=ROOM,

time: 80 us -> 78 us (0.975)
  the two profiles are of different devices: /device:TPU:6 before, /device:TPU:8 now
where the time goes in v6:
time: 78 us; the launch traced here: 77.5 us
  starting transfers between devices  36.3 us (47%)
  blocking collectives  25.8 us (33%)
  Pallas kernels  9.76 us (13%)
  waiting for transfers between devices  4.64 us (6%)
    all_gather x2, blocking collectives, gather(): lax.all_gather(block, ('core', 'sect'), axis=0, axis_index_groups=groups,...  13.9 us
    all_to_all x1, blocking collectives, local(): aggregate = lax.all_to_all(aggregate, 'sect', 0, 0)  11.9 us
    all_to_all x1, starting transfers between devices, local(): wanted = lax.all_to_all(wanted, 'z', 0, 0)  10.3 us
    pallas_call x7, Pallas kernels, call(): pl.pallas_call(kernel, out_shape=[jax.ShapeDtypeStruct(shape, kind) for s...  9.76 us
    all_to_all x1, starting transfers between devices, local(): offered = lax.all_to_all(offered, ('core', 'y'), 0, 0).reshape(-1, share)  7.56 us
    all_to_all x1, starting transfers between devices, local(): halo = lax.all_to_all(halo, 'z', 0, 0)  7.19 us
    ppermute x2, starting transfers between devices, local(): lax.ppermute(side, ('core', 'sect'), to)  6.59 us
    ppermute x1, starting transfers between devices, local(): others = lax.ppermute(passed, ('core', 'sect'), second)  4.67 us
  transfers between devices with their start and end apart: 6, of which 2 were waited for; matrix products, arithmetic and copies ran while one was open for 0% of the time, Pallas kernels for 7%

profile of v6, /device:TPU:8, one launch (start us, length us, event | category | flops | bytes accessed | tf_op | source)
XLA Modules:
  0.0 77.5 jit_solution(1089654968445114716)
XLA Ops:
  0.0 0.7 copy-done.11
  0.7 0.6 spread.1
  1.3 10.3 %all-to-all-start = ((s32[8,8,128]{2,1,0:T(8,128)}), s32[8,8,128]{2,1,0:T(8,128)S(1)}, u32[]{:S(2)}, u32[]{:S(2)}) async-start(s32[8,8,128]{2,1,0:T(8,128)} %spread.1), calls=%async_computation | async-start | bytes 65536 | tf_op jit(solution)/shard_map/all_to_all | solution.py:262
  11.7 5.6 %all-gather = bf16[1024,128]{1,0:T(8,128)(2,1)S(1)} all-gather(bf16[512,128]{1,0:T(8,128)(2,1)S(1)} %copy-done.2), channel_id=2, replica_groups={{0,1},{2,3},{4,7},{5,6},{8,9},{10,11},{12,15},{13,14},{16,17},{18,19},{..., dimensions={0}, use_global_device_ids=true | all-gather | bytes 393216 | tf_op jit(solution)/shard_map/all_gather | solution.py:85
  17.3 8.2 %all_gather.11.refs_1_.refs_0_ = bf16[4,512,128]{2,1,0:T(8,128)(2,1)S(1)} all-gather(bf16[2,512,128]{2,1,0:T(8,128)(2,1)S(1)} %bitcast.21), channel_id=1, replica_groups={{0,3},{1,2},{4,5},{7,6},{8,11},{9,10},{12,13},{15,14},{16,19},{17,18},{..., dimensions={0}, use_global_device_ids=true | all-gather | bytes 786432 | tf_op jit(solution)/shard_map/all_gather | solution.py:85
  25.6 0.0 copy-start.10
  25.6 0.0 copy-start.16
  25.6 1.2 %offer.1 = bf16[16,32,128]{2,1,0:T(8,128)(2,1)} custom-call(s32[1,32]{1,0:T(1,128)S(1)} %copy-done.14, bf16[4,512,128]{2,1,0:T(8,128)(2,1)S(1)} %all_gather.11.refs_1_.refs_0_, bf16[512,512]{1,0:T(8,128)(2,1)S(1)} %copy-done.8, f32[1,512]{1,0:T(1,128)S(1)} %bitcast.16, bf16[512,128]{1,0:T(8,128)(2,1)S(1)} %copy-done.9, f32[1,128]{1,0:T(1,128)S(1)} %bitcast.18), custom_call_target="tpu_custom_call" | custom-call | flops 10000000000 | tf_op jit(solution)/shard_map/offer/pallas_call | solution.py:53
  26.8 7.6 %all-to-all-start.1 = ((bf16[16,32,128]{2,1,0:T(8,128)(2,1)}), bf16[16,32,128]{2,1,0:T(8,128)(2,1)S(1)}, u32[]{:S(2)}, u32[]{:S(2)}) async-start(bf16[16,32,128]{2,1,0:T(8,128)(2,1)} %offer.1), calls=%async_computation.1 | async-start | bytes 262144 | tf_op jit(solution)/shard_map/all_to_all | solution.py:270
  34.4 0.8 %send.1 = (bf16[512,128]{1,0:T(8,128)(2,1)S(1)}, bf16[528,128]{1,0:T(8,128)(2,1)S(1)}) custom-call(bf16[4,512,128]{2,1,0:T(8,128)(2,1)S(1)} %all_gather.11.refs_1_.refs_0_, bf16[512,512]{1,0:T(8,128)(2,1)S(1)} %copy-done.8, f32[1,512]{1,0:T(1,128)S(1)} %bitcast.17, bf16[512,128]{1,0:T(8,128)(2,1)S(1)} %copy-done.9, f32[1,128]{1,0:T(1,128)S(1)} %bitcast.19, ...), custom_call_target="tpu_custom_call" | custom-call | flops 10000000000 | tf_op jit(solution)/shard_map/send/pallas_call | solution.py:53
  35.2 4.7 %collective-permute-start.1 = (bf16[528,128]{1,0:T(8,128)(2,1)S(1)}, bf16[528,128]{1,0:T(8,128)(2,1)S(1)}, u32[]{:S(2)}, u32[]{:S(2)}) collective-permute-start(bf16[528,128]{1,0:T(8,128)(2,1)S(1)} %get-tuple-element.27.refs_6_), channel_id=1, source_target_pairs={{0,3},{1,2},{2,1},{3,0},{4,5},{5,4},{6,7},{7,6},{8,11},{9,10},{10,... | collective-permute-start | bytes 405512 | tf_op jit(solution)/shard_map/ppermute | solution.py:283
  39.9 1.9 %collective-permute-start = (bf16[528,128]{1,0:T(8,128)(2,1)S(1)}, bf16[528,128]{1,0:T(8,128)(2,1)S(1)}, u32[]{:S(2)}, u32[]{:S(2)}) collective-permute-start(bf16[528,128]{1,0:T(8,128)(2,1)S(1)} %get-tuple-element.27.refs_6_), channel_id=1, source_target_pairs={{0,1},{1,0},{2,3},{3,2},{4,7},{5,6},{6,5},{7,4},{8,9},{9,8},{10,11... | collective-permute-start | bytes 405512 | tf_op jit(solution)/shard_map/ppermute | solution.py:283
  41.8 0.8 %all-to-all-done.1 = bf16[16,32,128]{2,1,0:T(8,128)(2,1)S(1)} async-done(((bf16[16,32,128]{2,1,0:T(8,128)(2,1)}), bf16[16,32,128]{2,1,0:T(8,128)(2,1)S(1)}, u32[]{:S(2)}, u32[]{:S(2)}) %all-to-all-start.1) | async-done | bytes 131104 | tf_op jit(solution)/shard_map/all_to_all | solution.py:270
  42.6 1.2 %select.1 = bf16[8,128,128]{2,1,0:T(8,128)(2,1)} custom-call(s32[8,8,128]{2,1,0:T(8,128)S(1)} %all-to-all-done.refs_0_, bf16[512,128]{1,0:T(8,128)(2,1)S(1)} %bitcast.11), custom_call_target="tpu_custom_call" | custom-call | flops 20000000000 | tf_op jit(solution)/shard_map/select/pallas_call | solution.py:53
  43.8 7.2 %all-to-all-start.2 = ((bf16[8,128,128]{2,1,0:T(8,128)(2,1)}), bf16[8,128,128]{2,1,0:T(8,128)(2,1)S(1)}, u32[]{:S(2)}, u32[]{:S(2)}) async-start(bf16[8,128,128]{2,1,0:T(8,128)(2,1)} %select.1), calls=%async_computation.2 | async-start | bytes 524288 | tf_op jit(solution)/shard_map/all_to_all | solution.py:293
  51.0 0.0 copy-start.13
  51.1 2.8 %above.1.refs_3_.refs_5_ = f32[512,512]{1,0:T(8,128)} custom-call(bf16[4,512,128]{2,1,0:T(8,128)(2,1)} %copy-done.3, bf16[1024,512]{1,0:T(8,128)(2,1)} %refs_0_.5), custom_call_target="tpu_custom_call" | custom-call | flops 10000000000 | tf_op jit(solution)/shard_map/above/pallas_call | solution.py:53
  53.9 4.7 %collective-permute-start.2 = (bf16[528,128]{1,0:T(8,128)(2,1)S(1)}, bf16[528,128]{1,0:T(8,128)(2,1)S(1)}, u32[]{:S(2)}, u32[]{:S(2)}) collective-permute-start(bf16[528,128]{1,0:T(8,128)(2,1)S(1)} %collective-permute-done.refs_7_), channel_id=1, source_target_pairs={{0,3},{1,2},{2,1},{3,0},{4,5},{5,4},{6,7},{7,6},{8,11},{9,10},{10,... | collective-permute-start | bytes 405512 | tf_op jit(solution)/shard_map/ppermute | solution.py:303
  58.6 3.9 %all-to-all-done.2.refs_2_ = bf16[8,128,128]{2,1,0:T(8,128)(2,1)S(1)} async-done(((bf16[8,128,128]{2,1,0:T(8,128)(2,1)}), bf16[8,128,128]{2,1,0:T(8,128)(2,1)S(1)}, u32[]{:S(2)}, u32[]{:S(2)}) %all-to-all-start.2) | async-done | bytes 262176 | tf_op jit(solution)/shard_map/all_to_all | solution.py:293
  62.4 0.0 copy-start.5
  62.4 0.0 copy-start.6
  62.5 1.3 %tiles.1 = bf16[4,512,128]{2,1,0:T(8,128)(2,1)S(1)} custom-call(s32[4,16]{1,0:T(4,128)S(1)} %copy-done.13, bf16[512,128]{1,0:T(8,128)(2,1)S(1)} %get-tuple-element.22.refs_1_, bf16[8,128,128]{2,1,0:T(8,128)(2,1)S(1)} %all-to-all-done.2.refs_2_, bf16[4,16,128,128]{3,2,1,0:T(8,128)(2,1)S(1)} %copy-done.7, bf16[4,16,128,128]{3,2,1,0:T(8,128)(2,1)S(1)} %copy-done.7, ...), custom_call_target="tpu_custom_call" | custom-call | flops 20000000000 | tf_op jit(solution)/shard_map/tiles/pallas_call | solution.py:53
  63.8 11.9 %all_to_all.20.refs_2_.refs_4_ = bf16[4,512,128]{2,1,0:T(8,128)(2,1)S(1)} all-to-all(bf16[4,512,128]{2,1,0:T(8,128)(2,1)S(1)} %tiles.1), channel_id=1, replica_groups=mesh['y'=8,'z'=8,'core'=2,'sect'=4] {'sect'}, dimensions={0} | all-to-all | bytes 1048576 | tf_op jit(solution)/shard_map/all_to_all | solution.py:317
  75.7 1.8 %node.1 = bf16[512,128]{1,0:T(8,128)(2,1)} custom-call(bf16[1024,512]{1,0:T(8,128)(2,1)S(1)} %copy-done.1, f32[1,512]{1,0:T(1,128)S(1)} %bitcast.12, bf16[4,512,128]{2,1,0:T(8,128)(2,1)S(1)} %all_to_all.20.refs_2_.refs_4_, f32[512,512]{1,0:T(8,128)S(1)} %copy-done, bf16[4,512,128]{2,1,0:T(8,128)(2,1)S(1)} %all_to_all.20.refs_2_.refs_4_, ...), custom_call_target="tpu_custom_call" | custom-call | tf_op jit(solution)/shard_map/node/pallas_call | solution.py:53
  (32 shorter events, 0.1 us)
Async XLA Ops:
  0.0 0.7 copy-start.11
  0.7 11.0 %copy-start.2 = (bf16[512,128]{1,0:T(8,128)(2,1)S(1)}, bf16[512,128]{1,0:T(8,128)(2,1)}, u32[]{:S(2)}) copy-start(bf16[512,128]{1,0:T(8,128)(2,1)} %refs_10_.1) | copy-start | bytes 393220
  0.7 24.9 %copy-start.8 = (bf16[512,512]{1,0:T(8,128)(2,1)S(1)}, bf16[512,512]{1,0:T(8,128)(2,1)}, u32[]{:S(2)}) copy-start(bf16[512,512]{1,0:T(8,128)(2,1)} %refs_1_.2) | copy-start | bytes 1572868
  0.7 24.9 %copy-start.9 = (bf16[512,128]{1,0:T(8,128)(2,1)S(1)}, bf16[512,128]{1,0:T(8,128)(2,1)}, u32[]{:S(2)}) copy-start(bf16[512,128]{1,0:T(8,128)(2,1)} %refs_3_.2) | copy-start | bytes 393220
  0.7 24.9 %copy-start.12 = (f32[512]{0:T(512)S(1)}, f32[512]{0:T(512)}, u32[]{:S(2)}) copy-start(f32[512]{0:T(512)} %param.21) | copy-start | bytes 6148
  0.7 24.9 %copy-start.14 = (s32[1,32]{1,0:T(1,128)S(1)}, s32[1,32]{1,0:T(1,128)}, u32[]{:S(2)}) copy-start(s32[1,32]{1,0:T(1,128)} %refs_0_.3) | copy-start | bytes 388
  0.7 24.9 %copy-start.15 = (f32[128]{0:T(128)S(1)}, f32[128]{0:T(128)}, u32[]{:S(2)}) copy-start(f32[128]{0:T(128)} %param.23) | copy-start | bytes 1540
  1.3 24.2 %all-to-all-start = ((s32[8,8,128]{2,1,0:T(8,128)}), s32[8,8,128]{2,1,0:T(8,128)S(1)}, u32[]{:S(2)}, u32[]{:S(2)}) async-start(s32[8,8,128]{2,1,0:T(8,128)} %spread.1), calls=%async_computation | async-start | bytes 65536 | tf_op jit(solution)/shard_map/all_to_all | solution.py:262
  25.6 8.8 %copy-start.3 = (bf16[4,512,128]{2,1,0:T(8,128)(2,1)}, bf16[4,512,128]{2,1,0:T(8,128)(2,1)S(1)}, u32[]{:S(2)}) copy-start(bf16[4,512,128]{2,1,0:T(8,128)(2,1)S(1)} %all_gather.11.refs_1_.refs_0_) | copy-start | bytes 1572868
  25.6 8.8 %copy-start.10 = (bf16[512,128]{1,0:T(8,128)(2,1)S(1)}, bf16[512,128]{1,0:T(8,128)(2,1)}, u32[]{:S(2)}) copy-start(bf16[512,128]{1,0:T(8,128)(2,1)} %refs_5_.2) | copy-start | bytes 393220
  25.6 8.8 %copy-start.16 = (bf16[128]{0:T(256)(128)(2,1)S(1)}, bf16[128]{0:T(256)(128)(2,1)}, u32[]{:S(2)}) copy-start(bf16[128]{0:T(256)(128)(2,1)} %param.27) | copy-start | bytes 772
  26.8 15.8 %all-to-all-start.1 = ((bf16[16,32,128]{2,1,0:T(8,128)(2,1)}), bf16[16,32,128]{2,1,0:T(8,128)(2,1)S(1)}, u32[]{:S(2)}, u32[]{:S(2)}) async-start(bf16[16,32,128]{2,1,0:T(8,128)(2,1)} %offer.1), calls=%async_computation.1 | async-start | bytes 262144 | tf_op jit(solution)/shard_map/all_to_all | solution.py:270
  35.2 15.8 %collective-permute-start.1 = (bf16[528,128]{1,0:T(8,128)(2,1)S(1)}, bf16[528,128]{1,0:T(8,128)(2,1)S(1)}, u32[]{:S(2)}, u32[]{:S(2)}) collective-permute-start(bf16[528,128]{1,0:T(8,128)(2,1)S(1)} %get-tuple-element.27.refs_6_), channel_id=1, source_target_pairs={{0,3},{1,2},{2,1},{3,0},{4,5},{5,4},{6,7},{7,6},{8,11},{9,10},{10,... | collective-permute-start | bytes 405512 | tf_op jit(solution)/shard_map/ppermute | solution.py:283
  39.9 11.1 %collective-permute-start = (bf16[528,128]{1,0:T(8,128)(2,1)S(1)}, bf16[528,128]{1,0:T(8,128)(2,1)S(1)}, u32[]{:S(2)}, u32[]{:S(2)}) collective-permute-start(bf16[528,128]{1,0:T(8,128)(2,1)S(1)} %get-tuple-element.27.refs_6_), channel_id=1, source_target_pairs={{0,1},{1,0},{2,3},{3,2},{4,7},{5,6},{6,5},{7,4},{8,9},{9,8},{10,11... | collective-permute-start | bytes 405512 | tf_op jit(solution)/shard_map/ppermute | solution.py:283
  43.8 18.6 %all-to-all-start.2 = ((bf16[8,128,128]{2,1,0:T(8,128)(2,1)}), bf16[8,128,128]{2,1,0:T(8,128)(2,1)S(1)}, u32[]{:S(2)}, u32[]{:S(2)}) async-start(bf16[8,128,128]{2,1,0:T(8,128)(2,1)} %select.1), calls=%async_computation.2 | async-start | bytes 524288 | tf_op jit(solution)/shard_map/all_to_all | solution.py:293
  51.0 11.4 %copy-start.7 = (bf16[4,16,128,128]{3,2,1,0:T(8,128)(2,1)S(1)}, bf16[4,16,128,128]{3,2,1,0:T(8,128)(2,1)}, u32[]{:S(2)}) copy-start(bf16[4,16,128,128]{3,2,1,0:T(8,128)(2,1)} %refs_6_.1) | copy-start | bytes 6291460
  51.0 11.4 %copy-start.13 = (s32[4,16]{1,0:T(4,128)S(1)}, s32[4,16]{1,0:T(4,128)}, u32[]{:S(2)}) copy-start(s32[4,16]{1,0:T(4,128)} %refs_0_.4) | copy-start | bytes 772
  53.9 9.9 %collective-permute-start.2 = (bf16[528,128]{1,0:T(8,128)(2,1)S(1)}, bf16[528,128]{1,0:T(8,128)(2,1)S(1)}, u32[]{:S(2)}, u32[]{:S(2)}) collective-permute-start(bf16[528,128]{1,0:T(8,128)(2,1)S(1)} %collective-permute-done.refs_7_), channel_id=1, source_target_pairs={{0,3},{1,2},{2,1},{3,0},{4,5},{5,4},{6,7},{7,6},{8,11},{9,10},{10,... | collective-permute-start | bytes 405512 | tf_op jit(solution)/shard_map/ppermute | solution.py:303
  62.4 13.3 %copy-start = (f32[512,512]{1,0:T(8,128)S(1)}, f32[512,512]{1,0:T(8,128)}, u32[]{:S(2)}) copy-start(f32[512,512]{1,0:T(8,128)} %above.1.refs_3_.refs_5_) | copy-start | bytes 3145732
  62.4 13.3 %copy-start.1 = (bf16[1024,512]{1,0:T(8,128)(2,1)S(1)}, bf16[1024,512]{1,0:T(8,128)(2,1)}, u32[]{:S(2)}) copy-start(bf16[1024,512]{1,0:T(8,128)(2,1)} %refs_0_.5) | copy-start | bytes 3145732
  62.4 13.3 %copy-start.4 = (f32[512]{0:T(512)S(1)}, f32[512]{0:T(512)}, u32[]{:S(2)}) copy-start(f32[512]{0:T(512)} %param.25) | copy-start | bytes 6148
  62.4 13.3 %copy-start.5 = (f32[128]{0:T(128)S(1)}, f32[128]{0:T(128)}, u32[]{:S(2)}) copy-start(f32[128]{0:T(128)} %param.28) | copy-start | bytes 1540
  62.4 13.3 %copy-start.6 = (f32[128]{0:T(128)S(1)}, f32[128]{0:T(128)}, u32[]{:S(2)}) copy-start(f32[128]{0:T(128)} %param.29) | copy-start | bytes 1540
